TPU v7x, 32 devices: a whole 2x2x4 slice. The times are simulated.
32 devices in a mesh: blk: 8 (over y, x, core), space: 4 (over z).
Axes of the slice: x: 2, y: 2, z: 4, core: 2. Of those that a mesh axis runs over, the one named last changes fastest.
Arguments:
- input_field: bfloat16 [128, 96, 96, 192], P('blk', 'space'), may hold values from -6 to 6
- cotangent: bfloat16 [128, 96, 96, 192], P('blk', 'space'), may hold values from -0.59765625 to 0.59765625
- weights: bfloat16 [16, 32, 8, 2, 128, 128], P('space', 'blk'), may hold values from -0.375 to 0.375
Outputs:
- spectral_out: bfloat16 [128, 96, 96, 192], P('blk', 'space')
- field_grad: bfloat16 [128, 96, 96, 192], P('blk', 'space')
- weight_grad: float32 [16, 32, 8, 2, 128, 128], P('space', 'blk')
All inputs are finite; a program needn't handle non-finite values.
Results may differ from a plain program's by a relative error of at most 0.015.
Values may be sent and summed in bfloat16 or wider, within the bound.
A program may use at most 192 MiB of HBM per device.

v0:
```python
import math

import jax
import jax.numpy as jnp
from jax import lax
from jax.sharding import PartitionSpec as P

NX = 96
NY = 192
NZ = 96
MX = 16
MY = 32
MZ = 8


def centered_freqs(total_count):
    indices = jnp.arange(total_count, dtype=jnp.int32)
    return jnp.where(indices < total_count // 2, indices, indices - total_count)


def phase_pair(frequencies, positions, length):
    product = frequencies[:, None] * positions[None, :] % length
    angles = product.astype(jnp.float32) * (2.0 * math.pi / length)
    return (jnp.cos(angles), jnp.sin(angles))


def x_analysis_table():
    cosines, sine_values = phase_pair(centered_freqs(MX), jnp.arange(NX, dtype=jnp.int32), NX)
    return jnp.stack([cosines.T, -sine_values.T], 1).astype(jnp.bfloat16)


def y_analysis_table():
    cosines, sine_values = phase_pair(centered_freqs(MY), jnp.arange(NY, dtype=jnp.int32), NY)
    real_rows = jnp.stack([cosines.T, -sine_values.T], 1)
    imag_rows = jnp.stack([sine_values.T, cosines.T], 1)
    return jnp.stack([real_rows, imag_rows], 0).astype(jnp.bfloat16)


def z_analysis_table(positions):
    cosines, sine_values = phase_pair(jnp.arange(MZ, dtype=jnp.int32), positions, NZ)
    real_rows = jnp.stack([cosines.T, -sine_values.T], 1)
    imag_rows = jnp.stack([sine_values.T, cosines.T], 1)
    return jnp.stack([real_rows, imag_rows], 0).astype(jnp.bfloat16)


def mode_weights():
    return jnp.where(jnp.arange(MZ) == 0, 1.0, 2.0).astype(jnp.float32)


def z_synthesis_table(positions, amplitude):
    cosines, sine_values = phase_pair(jnp.arange(MZ, dtype=jnp.int32), positions, NZ)
    cosines = cosines * amplitude[:, None]
    sine_values = sine_values * amplitude[:, None]
    real_rows = jnp.stack([cosines, sine_values], -1)
    imag_rows = jnp.stack([-sine_values, cosines], -1)
    return jnp.stack([real_rows, imag_rows], 1).astype(jnp.bfloat16)


def y_synthesis_table():
    cosines, sine_values = phase_pair(centered_freqs(MY), jnp.arange(NY, dtype=jnp.int32), NY)
    real_rows = jnp.stack([cosines, sine_values], 1)
    imag_rows = jnp.stack([-sine_values, cosines], 1)
    return jnp.stack([real_rows, imag_rows], 0).astype(jnp.bfloat16)


def x_synthesis_table():
    cosines, sine_values = phase_pair(centered_freqs(MX), jnp.arange(NX, dtype=jnp.int32), NX)
    return jnp.stack([cosines, -sine_values], 0).astype(jnp.bfloat16)


def contract(pattern, first_operand, second_operand):
    return jnp.einsum(pattern, first_operand, second_operand, preferred_element_type=jnp.float32)


def analyse(values, x_table, y_table):
    xsum = contract("czxy,xrp->czrpy", values, x_table).astype(jnp.bfloat16)
    return contract("czrpy,ryoq->czopq", xsum, y_table).astype(jnp.bfloat16)


def synthesize(zback, y_table, x_table):
    yback = contract("czipq,iqoy->czopy", zback, y_table).astype(jnp.bfloat16)
    return contract("czipy,ipx->czxy", yback, x_table).astype(jnp.bfloat16)


def scale_spectra(zsum_f, zsum_g, amplitude, forward_scale, synth_scale):
    spec_f = (zsum_f * forward_scale).astype(jnp.bfloat16)
    spec_g = (zsum_g * (amplitude * synth_scale)[None, :, None, None, None]).astype(jnp.bfloat16)
    return (spec_f, spec_g)


def shards(input_field, cotangent, weights):
    forward_scale = 1.0 / math.sqrt(NX * NY * NZ)
    synth_scale = 1.0 / math.sqrt(MX * MY * MZ)
    amplitude = mode_weights()
    unit_weights = jnp.ones((MZ,), jnp.float32)
    space_count = lax.axis_size("space")
    space_index = lax.axis_index("space")
    px_local = MX // space_count
    x_table = x_analysis_table()
    y_table = y_analysis_table()
    plane_f = analyse(input_field, x_table, y_table)
    plane_g = analyse(cotangent, x_table, y_table)
    pieces = (
        lax.all_gather(plane_f, "space", axis=1, tiled=True),
        lax.all_gather(plane_g, "space", axis=1, tiled=True),
    )
    row_count = pieces[0].shape[1]
    z_table = z_analysis_table(jnp.arange(row_count, dtype=jnp.int32))
    own_f = lax.dynamic_slice_in_dim(pieces[0], space_index * px_local, px_local, 3)
    own_g = lax.dynamic_slice_in_dim(pieces[1], space_index * px_local, px_local, 3)
    zsum_f = contract("czipq,izok->ckopq", own_f, z_table)
    zsum_g = contract("czipq,izok->ckopq", own_g, z_table)
    spec_f, spec_g = scale_spectra(zsum_f, zsum_g, amplitude, forward_scale, synth_scale)
    modes_f, modes_g = (
        lax.all_to_all(spec_f, "blk", split_axis=4, concat_axis=0, tiled=True),
        lax.all_to_all(spec_g, "blk", split_axis=4, concat_axis=0, tiled=True),
    )
    w_real = weights[:, :, :, 0]
    w_imag = weights[:, :, :, 1]
    f_real = modes_f[:, :, 0]
    f_imag = modes_f[:, :, 1]
    g_real = modes_g[:, :, 0]
    g_imag = modes_g[:, :, 1]
    mixed_real = contract("abkoc,ckab->okab", w_real, f_real) - contract(
        "abkoc,ckab->okab", w_imag, f_imag
    )
    mixed_imag = contract("abkoc,ckab->okab", w_real, f_imag) + contract(
        "abkoc,ckab->okab", w_imag, f_real
    )
    mixed = jnp.stack([mixed_real, mixed_imag], 2).astype(jnp.bfloat16)
    grad_real = contract("abkoc,okab->ckab", w_real, g_real) + contract(
        "abkoc,okab->ckab", w_imag, g_imag
    )
    grad_imag = contract("abkoc,okab->ckab", w_real, g_imag) - contract(
        "abkoc,okab->ckab", w_imag, g_real
    )
    grad_spec = jnp.stack([grad_real, grad_imag], 2).astype(jnp.bfloat16)
    wgrad_real = contract("okab,ckab->abkoc", g_real, f_real) + contract(
        "okab,ckab->abkoc", g_imag, f_imag
    )
    wgrad_imag = contract("okab,ckab->abkoc", g_imag, f_real) - contract(
        "okab,ckab->abkoc", g_real, f_imag
    )
    weight_grad = jnp.stack([wgrad_real, wgrad_imag], 3)
    all_positions = jnp.arange(NZ, dtype=jnp.int32)
    back_y, back_u = (
        lax.all_to_all(mixed, "blk", split_axis=0, concat_axis=4, tiled=True),
        lax.all_to_all(grad_spec, "blk", split_axis=0, concat_axis=4, tiled=True),
    )
    spread_y = (
        contract("ckipq,kizo->czopq", back_y, z_synthesis_table(all_positions, amplitude))
        * synth_scale
    ).astype(jnp.bfloat16)
    spread_u = (
        contract("ckipq,kizo->czopq", back_u, z_synthesis_table(all_positions, unit_weights))
        * forward_scale
    ).astype(jnp.bfloat16)
    zback_y, zback_u = (
        lax.all_to_all(spread_y, "space", split_axis=1, concat_axis=3, tiled=True),
        lax.all_to_all(spread_u, "space", split_axis=1, concat_axis=3, tiled=True),
    )
    y_back_table = y_synthesis_table()
    x_back_table = x_synthesis_table()
    spectral_out = synthesize(zback_y, y_back_table, x_back_table)
    field_grad = synthesize(zback_u, y_back_table, x_back_table)
    return (spectral_out, field_grad, weight_grad)


def solution(mesh):
    placed = (
        P("blk", "space", None, None),
        P("blk", "space", None, None),
        P("space", "blk", None, None, None, None),
    )
    return jax.shard_map(
        shards,
        mesh=mesh,
        in_specs=placed,
        out_specs=(
            P("blk", "space", None, None),
            P("blk", "space", None, None),
            P("space", "blk", None, None, None, None),
        ),
        check_vma=False,
    )
```

profile of v0, /device:TPU:0, one launch (start us, length us, event | category | flops | bytes accessed | tf_op | source)
XLA Modules:
  0.0 641.1 jit_solution(4574776586978885350)
XLA Ops:
  7.6 7.8 %convert_bitcast_fusion.1 = bf16[16,24,2,16,192,1]{4,3,1,0,2,5:T(8,128)(2,1)S(1)} fusion(bf16[16,24,96,192]{3,2,1,0:T(8,128)(2,1)} %param.3, bf16[96,1,16]{0,2,1:T(8,128)(2,1)S(1)} %get-tuple-element.37, bf16[96,1,16]{0,2,1:T(8,128)(2,1)S(1)} %get-tuple-element.36), kind=kOutput, calls=%fused_computation.24 | convolution fusion | flops 455356416 | bytes 18880512 | tf_op jit(solution)/shard_map/czxy,xrp->czrpy/dot_general | solution.py:72
  21.6 7.8 %convert_bitcast_fusion = bf16[16,24,2,16,192,1]{4,3,1,0,2,5:T(8,128)(2,1)S(1)} fusion(bf16[16,24,96,192]{3,2,1,0:T(8,128)(2,1)} %param.4, bf16[96,1,16]{0,2,1:T(8,128)(2,1)S(1)} %get-tuple-element.37, bf16[96,1,16]{0,2,1:T(8,128)(2,1)S(1)} %get-tuple-element.36), kind=kOutput, calls=%fused_computation.23 | convolution fusion | flops 455356416 | bytes 18880512 | tf_op jit(solution)/shard_map/czxy,xrp->czrpy/dot_general | solution.py:72
  35.3 6.9 %slice_bitcast_fusion.1 = (bf16[4,4,8,128,128]{4,3,2,1,0:T(8,128)(2,1)}, bf16[4,4,8,128,128]{4,3,2,1,0:T(8,128)(2,1)}) fusion(bf16[4,4,8,2,128,128]{5,4,3,2,1,0:T(8,128)(2,1)} %param.5), kind=kLoop, calls=%fused_computation.28 | loop fusion | bytes 16777216 | tf_op jit(solution)/shard_map/squeeze | solution.py:118
  42.2 199.9 %all-gather.3.cloned.1.call-done = bf16[16,96,2,16,32]{4,3,2,0,1:T(8,128)(2,1)} async-done(((bf16[16,24,2,16,32]{4,3,2,0,1:T(8,128)(2,1)}), bf16[16,96,2,16,32]{4,3,2,0,1:T(8,128)(2,1)}) %all-gather.3.cloned.1.call-update) | async-done | bytes 3145744 | tf_op jit(solution)/shard_map/all_gather | solution.py:104
  242.1 218.6 %all-gather.5.cloned.1.call-done = bf16[16,96,2,16,32]{4,3,2,0,1:T(8,128)(2,1)} async-done(((bf16[16,24,2,16,32]{4,3,2,0,1:T(8,128)(2,1)}), bf16[16,96,2,16,32]{4,3,2,0,1:T(8,128)(2,1)}) %all-gather.5.cloned.1.call-update) | async-done | bytes 3145744 | tf_op jit(solution)/shard_map/all_gather | solution.py:105
  460.7 10.2 %constant_dynamic-slice_fusion = (bf16[16,96,2,4,32]{4,3,2,0,1:T(4,128)(2,1)}, bf16[16,96,2,4,32]{4,3,2,0,1:T(4,128)(2,1)S(1)}) fusion(bf16[16,96,2,16,32]{4,3,2,0,1:T(8,128)(2,1)} %all-gather.5.cloned.1.call-done, s32[]{:T(128)S(6)} %select_n.240, bf16[16,96,2,16,32]{4,3,2,0,1:T(8,128)(2,1)} %all-gather.3.cloned.1.call-done), kind=kLoop, calls=%fused_computation.187 | loop fusion | bytes 3145732 | tf_op jit(solution)/shard_map/dynamic_slice | solution.py:110
  470.8 5.4 copy.155
  485.8 4.4 copy.154
  494.4 4.4 all-to-all-start
  508.7 4.6 fusion.36
  522.8 4.4 all-to-all-start.4
  540.0 5.2 copy.89
  549.0 4.2 all-to-all-start.5
  558.0 5.2 copy.73
  567.1 7.2 %all-to-all-done.5 = bf16[4,2,49152]{2,1,0:T(2,128)(2,1)} async-done(((bf16[4,2,49152]{2,1,0:T(2,128)(2,1)}), bf16[4,2,49152]{2,1,0:T(2,128)(2,1)}, u32[]{:S(2)}, u32[]{:S(2)}) %all-to-all-start.5) | async-done | bytes 786464 | tf_op jit(solution)/shard_map/all_to_all | solution.py:160
  574.3 4.6 all-to-all-start.2
  578.9 4.7 add_bitcast_fusion
  583.6 6.2 pad_maximum_fusion
  589.8 4.5 reshape.675
  594.3 5.5 copy.91
  599.9 4.5 reshape.669
  604.4 7.2 %copy.75 = bf16[16,24,2,4,4,32]{5,1,4,3,2,0:T(8,128)(2,1)} copy(bf16[16,24,2,4,4,32]{5,4,0,2,1,3:T(4,128)(2,1)} %bitcast.339) | data formatting | bytes 1572864 | tf_op jit(solution)/shard_map/all_to_all | solution.py:159
  611.5 10.4 %fusion.1 = bf16[16,24,96,192]{3,2,1,0:T(8,128)(2,1)} fusion(bf16[16,24,2,16,32,1]{4,1,3,2,0,5:T(8,128)(2,1)S(1)} %bitcast.336, bf16[1,32,2,192]{3,1,0,2:T(8,128)(2,1)S(1)} %get-tuple-element.16, bf16[1,32,2,192]{3,1,0,2:T(8,128)(2,1)S(1)} %get-tuple-element.15, bf16[1,16,96]{2,1,0:T(8,128)(2,1)S(1)} %get-tuple-element.26, ...), kind=kOutput, calls=%fused_computation.3 | convolution fusion | flops 764522496 | bytes 14997504 | tf_op jit(solution)/shard_map/czipy,ipx->czxy/dot_general | solution.py:72
  621.9 12.1 %fusion = bf16[16,24,96,192]{3,2,1,0:T(8,128)(2,1)} fusion(bf16[16,24,2,16,32,1]{4,1,3,2,0,5:T(8,128)(2,1)} %bitcast.337, bf16[1,32,2,192]{3,1,0,2:T(8,128)(2,1)S(1)} %get-tuple-element.16, bf16[1,32,2,192]{3,1,0,2:T(8,128)(2,1)S(1)} %get-tuple-element.15, bf16[1,16,96]{2,1,0:T(8,128)(2,1)S(1)} %get-tuple-element.26, ...), kind=kOutput, calls=%fused_computation.2 | convolution fusion | flops 764522496 | bytes 14997504 | tf_op jit(solution)/shard_map/czipy,ipx->czxy/dot_general | solution.py:72
  (82 shorter events, 70.5 us)
Async XLA Ops:
  7.2 234.9 %all-gather.3.cloned.1.call-start = ((), (), s32[]{:S(2)}) async-start(), calls=%async_computation.6 | async-start | bytes 15728640 | tf_op jit(solution)/shard_map/all_gather | solution.py:104
  21.0 439.6 %all-gather.5.cloned.1.call-start = ((), (), s32[]{:S(2)}) async-start(), calls=%async_computation.7 | async-start | bytes 15728640 | tf_op jit(solution)/shard_map/all_gather | solution.py:105
  482.1 12.2 %all-to-all-start.3 = ((bf16[8,2,2048]{2,1,0:T(2,128)(2,1)}), bf16[8,2,2048]{2,1,0:T(2,128)(2,1)S(1)}, u32[]{:S(2)}, u32[]{:S(2)}) async-start(bf16[8,2,2048]{2,1,0:T(2,128)(2,1)} %reshape.670), calls=%async_computation.3 | async-start | bytes 131072 | tf_op jit(solution)/shard_map/all_to_all | solution.py:116
  494.4 12.9 %all-to-all-start = ((bf16[8,2,2048]{2,1,0:T(2,128)(2,1)}), bf16[8,2,2048]{2,1,0:T(2,128)(2,1)S(1)}, u32[]{:S(2)}, u32[]{:S(2)}) async-start(bf16[8,2,2048]{2,1,0:T(2,128)(2,1)} %reshape.664), calls=%async_computation | async-start | bytes 131072 | tf_op jit(solution)/shard_map/all_to_all | solution.py:115
  500.1 3.6 copy-start
  500.1 4.7 copy-start.2
  508.6 4.6 copy-start.3
  513.3 4.6 copy-start.1
  522.8 9.4 %all-to-all-start.4 = ((bf16[8,2,2048]{2,1,0:T(2,128)(2,1)}), bf16[8,2,2048]{2,1,0:T(2,128)(2,1)S(1)}, u32[]{:S(2)}, u32[]{:S(2)}) async-start(bf16[8,2,2048]{2,1,0:T(2,128)(2,1)} %reshape.672), calls=%async_computation.4 | async-start | bytes 131072 | tf_op jit(solution)/shard_map/all_to_all | solution.py:148
  532.2 16.8 %all-to-all-start.1 = ((bf16[8,2,2048]{2,1,0:T(2,128)(2,1)}), bf16[8,2,2048]{2,1,0:T(2,128)(2,1)S(1)}, u32[]{:S(2)}, u32[]{:S(2)}) async-start(bf16[8,2,2048]{2,1,0:T(2,128)(2,1)} %reshape.666), calls=%async_computation.1 | async-start | bytes 131072 | tf_op jit(solution)/shard_map/all_to_all | solution.py:147
  549.0 25.2 %all-to-all-start.5 = ((bf16[4,2,49152]{2,1,0:T(2,128)(2,1)}), bf16[4,2,49152]{2,1,0:T(2,128)(2,1)}, u32[]{:S(2)}, u32[]{:S(2)}) async-start(bf16[4,2,49152]{2,1,0:T(2,128)(2,1)} %reshape.674), calls=%async_computation.5 | async-start | bytes 1572864 | tf_op jit(solution)/shard_map/all_to_all | solution.py:160
  574.3 25.6 %all-to-all-start.2 = ((bf16[4,2,49152]{2,1,0:T(2,128)(2,1)}), bf16[4,2,49152]{2,1,0:T(2,128)(2,1)}, u32[]{:S(2)}, u32[]{:S(2)}) async-start(bf16[4,2,49152]{2,1,0:T(2,128)(2,1)} %reshape.668), calls=%async_computation.2 | async-start | bytes 1572864 | tf_op jit(solution)/shard_map/all_to_all | solution.py:159
Sparse Core Ops, SparseCore 0:
  21.1 220.9 all-gather.2
  244.2 216.3 all-gather.4
where the time goes:
time: 646 us; the launch traced here: 641 us
  waiting for transfers between devices  428 us (66%)
  local copies, waits for them, and re-layouts  91.2 us (14%)
  matrix products  69.8 us (11%)
  starting transfers between devices  25.2 us (4%)
  between operations  14.6 us (2%)
  other arithmetic  12.3 us (2%)
    all_gather x1, waiting for transfers between devices, shards(): lax.all_gather(plane_g, 'space', axis=1, tiled=True)  219 us
    all_gather x1, waiting for transfers between devices, shards(): lax.all_gather(plane_f, 'space', axis=1, tiled=True)  200 us
    dot_general x18, matrix products, contract(): jnp.einsum(pattern, first_operand, second_operand, preferred_element_type...  69.8 us
    unnamed x22, local copies, waits for them, and re-layouts  36.5 us
  transfers between devices with their start and end apart: 8, of which 4 were waited for; matrix products, arithmetic and copies ran while one was open for 14% of the time, Pallas kernels for 0%

commit v1 on v0

v1 whole, which is shorter than its diff:
```python
import functools
import math

import jax
import jax.numpy as jnp
import numpy as np
from jax import lax
from jax.experimental import pallas as pl
from jax.experimental.pallas import tpu as pltpu
from jax.sharding import PartitionSpec as P

F32 = jnp.float32
BF16 = jnp.bfloat16


def centered_freqs(count):
    indices = np.arange(count, dtype=np.int64)
    return np.where(indices < count // 2, indices, indices - count)


def phase_pair(frequencies, positions, length):
    product = (frequencies[:, None] * positions[None, :]) % length
    angles = product.astype(np.float32) * np.float32(2.0 * math.pi / length)
    return np.cos(angles).astype(np.float32), np.sin(angles).astype(np.float32)


def rounded(table):
    return np.asarray(table, np.float32).astype(jnp.bfloat16)


def lane_slots(my):
    return max(1, 128 // my)


def lane_groups(my, local):
    return math.gcd(lane_slots(my), local)


def y_tables(ny, my, groups):
    cosines, sines = phase_pair(centered_freqs(my), np.arange(ny), ny)
    half = lane_slots(my) * my
    forward = np.zeros((groups, ny, 2 * half), np.float32)
    for i in range(groups):
        forward[i, :, i * my:(i + 1) * my] = cosines.T
        forward[i, :, half + i * my:half + (i + 1) * my] = -sines.T
    return rounded(forward), rounded(np.swapaxes(forward, 1, 2))


def x_tables(nx, mx):
    cosines, sines = phase_pair(centered_freqs(mx), np.arange(nx), nx)
    forward = np.concatenate([cosines, -sines], 0)
    backward = np.concatenate([cosines, sines], 0).T
    return rounded(forward), rounded(backward)


def z_tables(nz, mz, my, space_count, groups):
    cosines, sines = phase_pair(np.arange(mz), np.arange(nz), nz)
    local = nz // space_count
    per_group = local // groups
    amplitude = np.where(np.arange(mz) == 0, 1.0, 2.0).astype(np.float32)[:, None]

    def spread(weight):
        pair = np.stack([rounded(cosines * weight), rounded(sines * weight)], 1).astype(np.float32)
        pair = pair.reshape(mz, 2, space_count, groups, per_group)
        pair = pair.transpose(2, 4, 0, 1, 3)
        unused = (lane_slots(my) - groups) * my
        return np.pad(np.repeat(pair, my, axis=-1), ((0, 0),) * 4 + ((0, unused),))

    return spread(np.ones_like(amplitude)), spread(amplitude)


def dot(first, second, dims=((1,), (0,))):
    return lax.dot_general(first, second, (dims, ((), ())), preferred_element_type=F32)


def analyse_kernel(v_ref, ty_ref, tx_ref, zc_ref, o_ref, t_ref):
    groups, ny, lanes = ty_ref.shape
    half = lanes // 2
    my = o_ref.shape[-1]
    per_group, mz = zc_ref.shape[0], zc_ref.shape[1]
    mx, nx = tx_ref.shape[0] // 2, tx_ref.shape[1]
    total = None
    for i in range(groups):
        rows = v_ref[0, i * per_group:(i + 1) * per_group].reshape(per_group * nx, ny)
        part = dot(rows, ty_ref[i])
        total = part if total is None else total + part
    t_ref[...] = total.astype(BF16)
    real = [None] * mz
    imag = [None] * mz
    for j in range(per_group):
        u = dot(tx_ref[...], t_ref[j * nx:(j + 1) * nx, :])
        re = u[:mx, :half] - u[mx:, half:]
        im = u[mx:, :half] + u[:mx, half:]
        for k in range(mz):
            c = zc_ref[j, k, 0:1, :]
            s = zc_ref[j, k, 1:2, :]
            zr = re * c + im * s
            zi = im * c - re * s
            real[k] = zr if j == 0 else real[k] + zr
            imag[k] = zi if j == 0 else imag[k] + zi
    for k in range(mz):
        for part, value in enumerate((real[k], imag[k])):
            summed = value[:, :my]
            for i in range(1, groups):
                summed = summed + value[:, i * my:(i + 1) * my]
            o_ref[0, k, part] = summed


def analyse(values, ty, tx, zc, mx, my):
    c, nz, nx, ny = values.shape
    per_group, mz, lanes = zc.shape[0], zc.shape[1], zc.shape[-1]
    return pl.pallas_call(
        analyse_kernel,
        grid=(c,),
        in_specs=[
            pl.BlockSpec((1, nz, nx, ny), lambda i: (i, 0, 0, 0)),
            pl.BlockSpec(ty.shape, lambda i: (0, 0, 0)),
            pl.BlockSpec(tx.shape, lambda i: (0, 0)),
            pl.BlockSpec(zc.shape, lambda i: (0, 0, 0, 0)),
        ],
        out_specs=pl.BlockSpec((1, mz, 2, mx, my), lambda i: (i, 0, 0, 0, 0)),
        out_shape=jax.ShapeDtypeStruct((c, mz, 2, mx, my), F32),
        scratch_shapes=[pltpu.VMEM((per_group * nx, 2 * lanes), BF16)],
        compiler_params=pltpu.CompilerParams(vmem_limit_bytes=48 * 2**20),
        name="analysis",
    )(values, ty, tx, zc)


def mix_kernel(s_ref, w_ref, m_ref, wg_ref):
    mz, _, c, _ = w_ref.shape[2:]
    for k in range(mz):
        f2 = s_ref[0, 0, k, :, :c]
        g2 = s_ref[0, 0, k, :, c:]
        wk = w_ref[0, 0, k].reshape(2 * c, c)
        fm = dot(f2, wk, ((1,), (1,)))
        gm = dot(g2, wk)
        m_ref[0, 0, 0, k:k + 1, :] = fm[0:1, :c] - fm[1:2, c:]
        m_ref[0, 0, 1, k:k + 1, :] = fm[1:2, :c] + fm[0:1, c:]
        m_ref[0, 0, 2, k:k + 1, :] = gm[0:1]
        m_ref[0, 0, 3, k:k + 1, :] = gm[1:2]
        wg_ref[0, 0, k] = dot(g2, f2, ((0,), (0,))).reshape(2, c, c)


def mix(spectra, weights):
    a, b, mz, _, c, _ = weights.shape
    rows = spectra.shape[3]
    return pl.pallas_call(
        mix_kernel,
        grid=(a, b),
        in_specs=[
            pl.BlockSpec((1, 1, mz, rows, 3 * c), lambda i, j: (i, j, 0, 0, 0)),
            pl.BlockSpec((1, 1, mz, 2, c, c), lambda i, j: (i, j, 0, 0, 0, 0)),
        ],
        out_specs=[
            pl.BlockSpec((1, 1, 4, mz, c), lambda i, j: (i, j, 0, 0, 0)),
            pl.BlockSpec((1, 1, mz, 2, c, c), lambda i, j: (i, j, 0, 0, 0, 0)),
        ],
        out_shape=[
            jax.ShapeDtypeStruct((a, b, 4, mz, c), F32),
            jax.ShapeDtypeStruct((a, b, mz, 2, c, c), F32),
        ],
        compiler_params=pltpu.CompilerParams(vmem_limit_bytes=48 * 2**20),
        name="mixing",
    )(spectra, weights)


def synthesis_kernel(scale, m_ref, zc_ref, tx_ref, ty_ref, o_ref, t_ref):
    groups, lanes, ny = ty_ref.shape
    half = lanes // 2
    per_group, mz = zc_ref.shape[0], zc_ref.shape[1]
    nx = tx_ref.shape[0]
    for j in range(per_group):
        re = im = None
        for k in range(mz):
            c = zc_ref[j, k, 0:1, :]
            s = zc_ref[j, k, 1:2, :]
            mr = m_ref[0, k, 0].astype(F32)
            mi = m_ref[0, k, 1].astype(F32)
            zr = mr * c - mi * s
            zi = mi * c + mr * s
            re = zr if k == 0 else re + zr
            im = zi if k == 0 else im + zi
        re = re * scale
        im = im * scale
        upper = jnp.concatenate([re, im], 1)
        lower = jnp.concatenate([-im, re], 1)
        block = jnp.concatenate([upper, lower], 0).astype(BF16)
        t_ref[j * nx:(j + 1) * nx, :] = dot(tx_ref[...], block).astype(BF16)
    for i in range(groups):
        out = dot(t_ref[...], ty_ref[i])
        o_ref[0, i * per_group:(i + 1) * per_group] = out.astype(BF16).reshape(per_group, nx, ny)


def synthesize(spectra, zc, tx, ty, scale):
    c, mz, _, mx, lanes = spectra.shape
    per_group = zc.shape[0]
    groups, _, ny = ty.shape
    nx = tx.shape[0]
    nz = per_group * groups
    return pl.pallas_call(
        functools.partial(synthesis_kernel, scale),
        grid=(c,),
        in_specs=[
            pl.BlockSpec((1, mz, 2, mx, lanes), lambda i: (i, 0, 0, 0, 0)),
            pl.BlockSpec(zc.shape, lambda i: (0, 0, 0, 0)),
            pl.BlockSpec(tx.shape, lambda i: (0, 0)),
            pl.BlockSpec(ty.shape, lambda i: (0, 0, 0)),
        ],
        out_specs=pl.BlockSpec((1, nz, nx, ny), lambda i: (i, 0, 0, 0)),
        out_shape=jax.ShapeDtypeStruct((c, nz, nx, ny), BF16),
        scratch_shapes=[pltpu.VMEM((per_group * nx, 2 * lanes), BF16)],
        compiler_params=pltpu.CompilerParams(vmem_limit_bytes=48 * 2**20),
        name="synthesis",
    )(spectra, zc, tx, ty)


def shards(input_field, cotangent, weights):
    blk_count = lax.axis_size("blk")
    space_count = lax.axis_size("space")
    space_index = lax.axis_index("space")
    c_local, nz_local, nx, ny = input_field.shape
    px, qx, mz = weights.shape[:3]
    mx, my = px * space_count, qx * blk_count
    channels = c_local * blk_count
    nz = nz_local * space_count
    groups = lane_groups(my, nz_local)
    forward_scale = 1.0 / math.sqrt(nx * ny * nz)
    synth_scale = 1.0 / math.sqrt(mx * my * mz)
    amplitude = np.where(np.arange(mz) == 0, 1.0, 2.0).astype(np.float32)
    ty_in, ty_out = y_tables(ny, my, groups)
    tx_in, tx_out = x_tables(nx, mx)
    zc_unit, zc_amp = z_tables(nz, mz, my, space_count, groups)
    zc_unit = lax.dynamic_index_in_dim(jnp.asarray(zc_unit), space_index, 0, keepdims=False)
    zc_amp = lax.dynamic_index_in_dim(jnp.asarray(zc_amp), space_index, 0, keepdims=False)

    part_f = analyse(input_field, ty_in, tx_in, zc_unit, mx, my)
    part_g = analyse(cotangent, ty_in, tx_in, zc_unit, mx, my)
    parts = jnp.stack([part_f, part_g], 0).astype(BF16)
    parts = parts.reshape(2, c_local, mz, 2, space_count, px, blk_count, qx)
    send = parts.transpose(4, 6, 0, 2, 3, 5, 7, 1)
    send = send.reshape(space_count * blk_count, -1, 128)
    got = lax.all_to_all(send, ("space", "blk"), split_axis=0, concat_axis=0, tiled=True)
    got = got.reshape(space_count, blk_count, 2, mz, 2, px, qx, c_local)
    zsum = jnp.sum(got.astype(F32), 0)
    zsum = zsum.transpose(1, 3, 4, 5, 2, 0, 6).reshape(2, 2, px, qx, mz, channels)
    spec_f = (zsum[0] * forward_scale).astype(BF16)
    spec_g = (zsum[1] * (amplitude * np.float32(synth_scale))[:, None]).astype(BF16)
    row0 = jnp.concatenate([spec_f[0], spec_g[0], spec_g[1]], -1)
    row1 = jnp.concatenate([spec_f[1], spec_g[1], -spec_g[0]], -1)
    spectra = jnp.stack([row0, row1], 3)
    spectra = jnp.pad(spectra, ((0, 0),) * 3 + ((0, 14), (0, 0)))
    mixed, weight_grad = mix(spectra, weights)

    back = mixed.astype(BF16).reshape(px, qx, 2, 2, mz, blk_count, c_local)
    back = back.transpose(5, 2, 6, 4, 3, 0, 1).reshape(1, blk_count, -1, 128)
    back = jnp.broadcast_to(back, (space_count,) + back.shape[1:])
    back = back.reshape(space_count * blk_count, -1, 128)
    home = lax.all_to_all(back, ("space", "blk"), split_axis=0, concat_axis=0, tiled=True)
    home = home.reshape(space_count, blk_count, 2, c_local, mz, 2, px, qx)
    home = home.transpose(2, 3, 4, 5, 0, 6, 1, 7).reshape(2, c_local, mz, 2, mx, my)
    home = jnp.concatenate([home] * lane_slots(my), -1)
    spectral_out = synthesize(home[0], zc_amp, tx_out, ty_out, synth_scale)
    field_grad = synthesize(home[1], zc_unit, tx_out, ty_out, forward_scale)
    return (spectral_out, field_grad, weight_grad)


def solution(mesh):
    placed = (
        P("blk", "space", None, None),
        P("blk", "space", None, None),
        P("space", "blk", None, None, None, None),
    )
    return jax.shard_map(
        shards,
        mesh=mesh,
        in_specs=placed,
        out_specs=placed,
        check_vma=False,
    )
```

time: 646 us -> 204 us (0.32)
  waiting for transfers between devices: 428 us -> 0 us
  Pallas kernels: 0 us -> 79.2 us
  matrix products: 69.8 us -> 0 us
  blocking collectives: 0 us -> 41.1 us
  local copies, waits for them, and re-layouts: 91.2 us -> 66 us
  starting transfers between devices: 25.2 us -> 0 us
  between operations: 14.6 us -> 0.91 us
    all_gather x2 -> x0, waiting for transfers between devices: 418 us -> none  [the longest x1 219 us: shards(): lax.all_gather(plane_g, 'space', axis=1, tiled=True)]
    pallas_call x0 -> x5, Pallas kernels: none -> 79.2 us  [the longest x2 35.9 us: analyse(): pl.pallas_call(analyse_kernel, grid=(c,), in_specs=[pl.BlockSpec((1, nz,...]
    dot_general x18 -> x0, matrix products: 69.8 us -> none  [contract(): jnp.einsum(pattern, first_operand, second_operand, preferred_element_type...]
    all_to_all x0 -> x2, blocking collectives: none -> 41.1 us  [the longest x1 22.6 us: shards(): lax.all_to_all(send, ('space', 'blk'), split_axis=0, concat_axis=0, tiled...]
    unnamed x22 -> x14, local copies, waits for them, and re-layouts: 36.5 us -> 2.24 us
    all_to_all x6 -> x0, starting transfers between devices: 24.6 us -> none  [the longest x1 4.59 us: shards(): lax.all_to_all(spread_y, 'space', split_axis=1, concat_axis=3, tiled=True)]
    reshape x0 -> x5, local copies, waits for them, and re-layouts: none -> 22.7 us  [the longest x1 6.05 us: shards(): send = send.reshape(space_count * blk_count, -1, 128)]
    transpose x0 -> x2, local copies, waits for them, and re-layouts: none -> 21.5 us  [the longest x1 17.1 us: shards(): home.transpose(2, 3, 4, 5, 0, 6, 1, 7).reshape(2, c_local, mz, 2, mx, my)]
  transfers between devices with their start and end apart: 8 -> 0, of which waited for: 4 -> 0; matrix products, arithmetic and copies ran while one was open for 14% -> 0% of each run, Pallas kernels for 0% -> 0%
where the time goes in v1:
time: 204 us; the launch traced here: 202 us
  Pallas kernels  79.2 us (39%)
  local copies, waits for them, and re-layouts  66 us (32%)
  blocking collectives  41.1 us (20%)
  other arithmetic  14.9 us (7%)
    pallas_call x2, Pallas kernels, analyse(): pl.pallas_call(analyse_kernel, grid=(c,), in_specs=[pl.BlockSpec((1, nz,...  35.9 us
    pallas_call x2, Pallas kernels, synthesize(): pl.pallas_call(functools.partial(synthesis_kernel, scale), grid=(c,), in_...  27.3 us
    all_to_all x1, blocking collectives, shards(): lax.all_to_all(send, ('space', 'blk'), split_axis=0, concat_axis=0, tiled...  22.6 us
    all_to_all x1, blocking collectives, shards(): lax.all_to_all(back, ('space', 'blk'), split_axis=0, concat_axis=0, tiled...  18.4 us
    transpose x1, local copies, waits for them, and re-layouts, shards(): home.transpose(2, 3, 4, 5, 0, 6, 1, 7).reshape(2, c_local, mz, 2, mx, my)  17.1 us
    pallas_call x1, Pallas kernels, mix(): pl.pallas_call(mix_kernel, grid=(a, b), in_specs=[pl.BlockSpec((1, 1, mz,...  16.1 us
    another operation x2, local copies, waits for them, and re-layouts  6.95 us
    convert_element_type x1, local copies, waits for them, and re-layouts, shards(): zsum = jnp.sum(got.astype(F32), 0)  6.89 us

profile of v1, /device:TPU:0, one launch (start us, length us, event | category | flops | bytes accessed | tf_op | source)
XLA Modules:
  0.0 202.1 jit_solution(12942007718218021865)
XLA Ops:
  1.5 1.0 copy-done.1
  3.2 17.9 %analysis.3 = f32[16,8,2,16,32]{4,3,2,1,0:T(8,128)S(1)} custom-call(bf16[16,24,96,192]{3,2,1,0:T(8,128)(2,1)} %v_ref.3, bf16[4,192,256]{2,1,0:T(8,128)(2,1)S(1)} %copy-done.1, bf16[32,96]{1,0:T(8,128)(2,1)S(1)} %copy-done.4, f32[6,8,2,128]{3,2,1,0:T(2,128)S(1)} %get-tuple-element.18.zc_ref), custom_call_target="tpu_custom_call" | custom-call | tf_op jit(solution)/shard_map/analysis/pallas_call | solution.py:112
  21.1 1.2 convert.10
  22.3 3.0 %copy.51 = bf16[16,8,2,16,32]{0,1,4,3,2:T(8,128)(2,1)S(1)} copy(bf16[16,8,2,16,32]{4,3,2,1,0:T(8,128)(2,1)} %convert.10) | data formatting | bytes 524288 | tf_op jit(solution)/shard_map/convert.3
  25.4 17.9 %analysis.2 = f32[16,8,2,16,32]{4,3,2,1,0:T(8,128)S(1)} custom-call(bf16[16,24,96,192]{3,2,1,0:T(8,128)(2,1)} %v_ref.2, bf16[4,192,256]{2,1,0:T(8,128)(2,1)S(1)} %copy-done.2, bf16[32,96]{1,0:T(8,128)(2,1)S(1)} %copy-done.5, f32[6,8,2,128]{3,2,1,0:T(2,128)S(1)} %get-tuple-element.18.zc_ref), custom_call_target="tpu_custom_call" | custom-call | tf_op jit(solution)/shard_map/analysis/pallas_call | solution.py:112
  43.3 1.2 convert.9
  44.5 3.9 %copy.50 = bf16[16,8,2,16,32]{0,1,4,3,2:T(8,128)(2,1)} copy(bf16[16,8,2,16,32]{4,3,2,1,0:T(8,128)(2,1)} %convert.9) | data formatting | bytes 524288 | tf_op jit(solution)/shard_map/convert.4
  48.5 2.5 %maximum_bitcast_fusion = bf16[4,8,2,8,2,4,4,16]{7,3,6,1,5,0,4,2:T(8,128)(2,1)S(1)} fusion(bf16[1,16,8,2,4,4,8,4]{1,2,7,6,5,4,3,0:T(8,128)(2,1)S(1)} %bitcast.43, bf16[1,16,8,2,4,4,8,4]{1,2,7,6,5,4,3,0:T(8,128)(2,1)} %bitcast.44), kind=kLoop, calls=%fused_computation | loop fusion | flops 262144 | bytes 1048576 | tf_op jit(solution)/shard_map/transpose | solution.py:240
  51.0 4.4 %copy.52 = bf16[4,8,2,8,2,4,4,16]{7,6,5,4,3,2,1,0:T(4,128)(2,1)} copy(bf16[4,8,2,8,2,4,4,16]{7,3,6,1,5,0,4,2:T(8,128)(2,1)S(1)} %maximum_bitcast_fusion) | data formatting | bytes 1048576 | tf_op jit(solution)/shard_map/transpose | solution.py:240
  55.4 6.0 %reshape.46 = bf16[32,64,128]{2,1,0:T(8,128)(2,1)S(1)} reshape(bf16[4,8,2,8,2,4,4,16]{7,6,5,4,3,2,1,0:T(4,128)(2,1)} %copy.52) | data formatting | bytes 1048576 | tf_op jit(solution)/shard_map/reshape | solution.py:241
  61.4 22.6 %all_to_all.10 = bf16[32,64,128]{2,1,0:T(8,128)(2,1)S(1)} all-to-all(bf16[32,64,128]{2,1,0:T(8,128)(2,1)S(1)} %reshape.46), channel_id=1, replica_groups=mesh['blk'=8,'space'=4] {'space','blk'}, dimensions={0} | all-to-all | bytes 1048576 | tf_op jit(solution)/shard_map/all_to_all | solution.py:242
  84.1 6.9 %reshape.51 = f32[4,8,2,8,2,4,4,16]{7,6,5,4,3,2,1,0:T(4,128)} reshape(bf16[32,64,128]{2,1,0:T(8,128)(2,1)S(1)} %all_to_all.10) | data formatting | bytes 1572864 | tf_op jit(solution)/shard_map/convert_element_type | solution.py:244
  91.0 6.5 %reduce_sum.9 = f32[8,2,8,2,4,4,16]{6,5,4,3,2,1,0:T(4,128)S(1)} reduce(f32[4,8,2,8,2,4,4,16]{7,6,5,4,3,2,1,0:T(4,128)} %reshape.51, f32[]{:T(128)} %constant.30.clone.1), dimensions={0}, to_apply=%region_0.1 | reduce | flops 196608 | bytes 1310724 | tf_op jit(solution)/shard_map/reduce_sum | solution.py:244
  101.1 16.1 %mixing.1 = (f32[4,4,4,8,128]{4,3,2,1,0:T(8,128)S(1)}, f32[4,4,8,2,128,128]{5,4,3,2,1,0:T(8,128)}) custom-call(bf16[4,4,8,16,384]{4,3,2,1,0:T(8,128)(2,1)S(1)} %fusion.2.s_ref, bf16[4,4,8,2,128,128]{5,4,3,2,1,0:T(8,128)(2,1)} %w_ref.1), custom_call_target="tpu_custom_call" | custom-call | tf_op jit(solution)/shard_map/mixing/pallas_call | solution.py:147
  117.9 4.0 %copy.58 = bf16[4,4,2,2,8,8,16]{5,1,0,3,4,6,2:T(4,128)(2,1)S(1)} copy(bf16[4,4,2,2,8,8,16]{6,5,4,3,2,1,0:T(8,128)(2,1)S(1)} %reshape.47) | data formatting | bytes 262144 | tf_op jit(solution)/shard_map/reshape | solution.py:254
  121.9 0.9 copy.59
  122.9 18.4 %all_to_all.11 = bf16[32,64,128]{2,1,0:T(8,128)(2,1)S(1)} all-to-all(bf16[32,64,128]{2,1,0:T(8,128)(2,1)S(1)} %bitcast.45), channel_id=1, replica_groups=mesh['blk'=8,'space'=4] {'space','blk'}, dimensions={0} | all-to-all | bytes 1048576 | tf_op jit(solution)/shard_map/all_to_all | solution.py:258
  141.4 1.1 copy.60
  142.5 6.0 %reshape.49 = bf16[4,8,2,16,8,2,4,4]{1,0,7,6,5,4,3,2:T(4,128)(2,1)} reshape(bf16[32,64,128]{0,2,1:T(8,128)(2,1)S(1)} %copy.60) | data formatting | bytes 1048576 | tf_op jit(solution)/shard_map/reshape | solution.py:259
  148.5 17.1 %copy.61 = bf16[2,16,8,2,4,4,8,4]{1,2,7,6,5,4,3,0:T(8,128)(2,1)} copy(bf16[2,16,8,2,4,4,8,4]{6,4,7,5,3,2,1,0:T(4,128)(2,1)} %bitcast.39) | data formatting | bytes 1048576 | tf_op jit(solution)/shard_map/transpose | solution.py:260
  165.6 6.0 %copy.62 = bf16[2,16,8,2,16,32]{5,4,3,2,1,0:T(8,128)(2,1)S(1)} copy(bf16[2,16,8,2,16,32]{1,2,5,4,3,0:T(8,128)(2,1)} %bitcast.40) | data formatting | bytes 1048576 | tf_op jit(solution)/shard_map/reshape | solution.py:260
  171.7 2.1 %pad_maximum_fusion = bf16[2,16,8,2,16,128]{5,4,3,2,1,0:T(8,128)(2,1)S(1)} fusion(bf16[2,16,8,2,16,32]{5,4,3,2,1,0:T(8,128)(2,1)S(1)} %copy.62), kind=kLoop, calls=%fused_computation.4 | loop fusion | flops 8388608 | bytes 2621440 | tf_op jit(solution)/shard_map/concatenate | solution.py:261
  174.8 13.6 %synthesis.3 = bf16[16,24,96,192]{3,2,1,0:T(8,128)(2,1)} custom-call(bf16[16,8,2,16,128]{4,3,2,1,0:T(8,128)(2,1)S(1)} %get-tuple-element.7.m_ref, f32[6,8,2,128]{3,2,1,0:T(2,128)S(1)} %get-tuple-element.18.zc_ref, bf16[96,32]{1,0:T(8,128)(2,1)S(1)} %copy-done.3, bf16[4,256,192]{2,1,0:T(8,128)(2,1)S(1)} %copy-done), custom_call_target="tpu_custom_call" | custom-call | tf_op jit(solution)/shard_map/synthesis/pallas_call | solution.py:200
  188.5 13.6 %synthesis.2 = bf16[16,24,96,192]{3,2,1,0:T(8,128)(2,1)} custom-call(bf16[16,8,2,16,128]{4,3,2,1,0:T(8,128)(2,1)S(1)} %get-tuple-element.8.m_ref, f32[6,8,2,128]{3,2,1,0:T(2,128)S(1)} %get-tuple-element.17.zc_ref, bf16[96,32]{1,0:T(8,128)(2,1)S(1)} %copy-done.3, bf16[4,256,192]{2,1,0:T(8,128)(2,1)S(1)} %copy-done), custom_call_target="tpu_custom_call" | custom-call | tf_op jit(solution)/shard_map/synthesis/pallas_call | solution.py:200
  (33 shorter events, 6.8 us)
Async XLA Ops:
  1.5 1.0 copy-start.1
  2.5 0.7 copy-start.4
  21.1 4.3 %copy-start.2 = (bf16[4,192,256]{2,1,0:T(8,128)(2,1)S(1)}, bf16[4,192,256]{2,1,0:T(8,128)(2,1)}, u32[]{:S(2)}) copy-start(bf16[4,192,256]{2,1,0:T(8,128)(2,1)} %constant.35.clone.ty_ref) | copy-start | bytes 1179652
  21.1 4.3 %copy-start.5 = (bf16[32,96]{1,0:T(8,128)(2,1)S(1)}, bf16[32,96]{1,0:T(8,128)(2,1)}, u32[]{:S(2)}) copy-start(bf16[32,96]{1,0:T(8,128)(2,1)} %constant.36.clone.tx_ref) | copy-start | bytes 18436
  97.5 1.5 copy-start.6
  173.8 1.0 copy-start
  173.8 1.0 copy-start.3

commit v2 on v1

v2 whole, which is shorter than its diff:
```python
import functools
import math

import jax
import jax.numpy as jnp
import numpy as np
from jax import lax
from jax.experimental import pallas as pl
from jax.experimental.pallas import tpu as pltpu
from jax.sharding import PartitionSpec as P

F32 = jnp.float32
BF16 = jnp.bfloat16


def centered_freqs(count):
    indices = np.arange(count, dtype=np.int64)
    return np.where(indices < count // 2, indices, indices - count)


def phase_pair(frequencies, positions, length):
    product = (frequencies[:, None] * positions[None, :]) % length
    angles = product.astype(np.float32) * np.float32(2.0 * math.pi / length)
    return np.cos(angles).astype(np.float32), np.sin(angles).astype(np.float32)


def rounded(table):
    return np.asarray(table, np.float32).astype(jnp.bfloat16)


def lane_slots(my):
    return max(1, 128 // my)


def lane_groups(my, local):
    return math.gcd(lane_slots(my), local)


def y_tables(ny, my, groups):
    cosines, sines = phase_pair(centered_freqs(my), np.arange(ny), ny)
    half = lane_slots(my) * my
    forward = np.zeros((groups, ny, 2 * half), np.float32)
    for i in range(groups):
        forward[i, :, i * my:(i + 1) * my] = cosines.T
        forward[i, :, half + i * my:half + (i + 1) * my] = -sines.T
    return rounded(forward), rounded(np.swapaxes(forward, 1, 2))


def x_tables(nx, mx):
    cosines, sines = phase_pair(centered_freqs(mx), np.arange(nx), nx)
    forward = np.concatenate([cosines, -sines], 0)
    backward = np.concatenate([cosines, sines], 0).T
    return rounded(forward), rounded(backward)


def z_tables(nz, mz, my, space_count, groups):
    cosines, sines = phase_pair(np.arange(mz), np.arange(nz), nz)
    local = nz // space_count
    per_group = local // groups
    amplitude = np.where(np.arange(mz) == 0, 1.0, 2.0).astype(np.float32)[:, None]

    def spread(weight):
        pair = np.stack([rounded(cosines * weight), rounded(sines * weight)], 1).astype(np.float32)
        pair = pair.reshape(mz, 2, space_count, groups, per_group)
        pair = pair.transpose(2, 4, 0, 1, 3)
        unused = (lane_slots(my) - groups) * my
        return np.pad(np.repeat(pair, my, axis=-1), ((0, 0),) * 4 + ((0, unused),))

    return spread(np.ones_like(amplitude)), spread(amplitude)


def dot(first, second, dims=((1,), (0,))):
    return lax.dot_general(first, second, (dims, ((), ())), preferred_element_type=F32)


def every(start, count, stride):
    return pl.ds(start, count) if stride == 1 else pl.ds(start, count, stride=stride)


def analyse_kernel(f_ref, g_ref, ty_ref, tx_ref, zc_ref, o_ref, t_ref, zs_ref):
    groups, ny, lanes = ty_ref.shape
    half = lanes // 2
    space, blk, _, qx, width = o_ref.shape
    my = blk * qx
    per_group, mz = zc_ref.shape[0], zc_ref.shape[1]
    mx, nx = tx_ref.shape[0] // 2, tx_ref.shape[1]
    for h, v_ref in enumerate((f_ref, g_ref)):
        total = None
        for i in range(groups):
            rows = v_ref[0, i * per_group:(i + 1) * per_group].reshape(per_group * nx, ny)
            part = dot(rows, ty_ref[i])
            total = part if total is None else total + part
        t_ref[h] = total.astype(BF16)
        real = [None] * mz
        imag = [None] * mz
        for j in range(per_group):
            u = dot(tx_ref[...], t_ref[h, j * nx:(j + 1) * nx, :])
            re = u[:mx, :half] - u[mx:, half:]
            im = u[mx:, :half] + u[:mx, half:]
            for k in range(mz):
                c = zc_ref[j, k, 0:1, :]
                s = zc_ref[j, k, 1:2, :]
                zr = re * c + im * s
                zi = im * c - re * s
                real[k] = zr if j == 0 else real[k] + zr
                imag[k] = zi if j == 0 else imag[k] + zi
        for k in range(mz):
            zs_ref[every(4 * k + 2 * h, mx, 4 * mz), :] = real[k]
            zs_ref[every(4 * k + 2 * h + 1, mx, 4 * mz), :] = imag[k]
    flipped = zs_ref[...].T
    summed = flipped[:my]
    for i in range(1, half // my):
        summed = summed + flipped[i * my:(i + 1) * my]
    for s in range(space):
        for b in range(blk):
            o_ref[s, b, 0] = summed[b * qx:(b + 1) * qx, s * width:(s + 1) * width]


def analyse(first, second, ty, tx, zc, sent):
    c, nz, nx, ny = first.shape
    per_group, mz, half = zc.shape[0], zc.shape[1], zc.shape[-1]
    mx = tx.shape[0] // 2
    space, blk, _, qx, width = sent
    return pl.pallas_call(
        analyse_kernel,
        grid=(c,),
        in_specs=[
            pl.BlockSpec((1, nz, nx, ny), lambda i: (i, 0, 0, 0)),
            pl.BlockSpec((1, nz, nx, ny), lambda i: (i, 0, 0, 0)),
            pl.BlockSpec(ty.shape, lambda i: (0, 0, 0)),
            pl.BlockSpec(tx.shape, lambda i: (0, 0)),
            pl.BlockSpec(zc.shape, lambda i: (0, 0, 0, 0)),
        ],
        out_specs=pl.BlockSpec((space, blk, 1, qx, width), lambda i: (0, 0, i, 0, 0)),
        out_shape=jax.ShapeDtypeStruct(sent, F32),
        scratch_shapes=[
            pltpu.VMEM((2, per_group * nx, 2 * half), BF16),
            pltpu.VMEM((mx * mz * 4, half), F32),
        ],
        compiler_params=pltpu.CompilerParams(vmem_limit_bytes=48 * 2**20),
        name="analysis",
    )(first, second, ty, tx, zc)


def mix_kernel(s_ref, scale_ref, w_ref, o_ref, wg_ref, sum_ref, in_ref, out_ref):
    mz, _, c, _ = w_ref.shape[2:]
    qx = in_ref.shape[0]
    rows = 4 * mz
    a, j = pl.program_id(0), pl.program_id(1)

    @pl.when((a == 0) & (j == 0))
    def _():
        total = s_ref[0].astype(F32)
        for s in range(1, s_ref.shape[0]):
            total = total + s_ref[s].astype(F32)
        sum_ref[...] = total
        for i in range(qx):
            in_ref[i] = sum_ref[every(i, c, qx), :].T * scale_ref[...]

    start = pl.multiple_of(a * rows, 8)
    x = in_ref[j, pl.ds(start, rows), :]
    mixed = []
    for k in range(mz):
        fr, fi, gr, gi = (x[4 * k + i:4 * k + i + 1] for i in range(4))
        row0 = jnp.concatenate([fr, gr, gi], 1)
        row1 = jnp.concatenate([fi, gi, -gr], 1)
        both = jnp.concatenate([row0, row1, jnp.zeros((14, 3 * c), F32)], 0).astype(BF16)
        f2 = both[:, :c]
        g2 = both[:, c:]
        wk = w_ref[0, 0, k].reshape(2 * c, c)
        fm = dot(f2, wk, ((1,), (1,)))
        gm = dot(g2, wk)
        mixed += [fm[0:1, :c] - fm[1:2, c:], fm[1:2, :c] + fm[0:1, c:], gm[0:2]]
        wg_ref[0, 0, k] = dot(g2, f2, ((0,), (0,))).reshape(2, c, c)
    out_ref[j, pl.ds(start, rows), :] = jnp.concatenate(mixed, 0)

    @pl.when((a == pl.num_programs(0) - 1) & (j == pl.num_programs(1) - 1))
    def _():
        for i in range(qx):
            o_ref[every(i, c, qx), :] = out_ref[i].T


def mix(spectra, scales, weights):
    a, b, mz, _, c, _ = weights.shape
    rows, width = spectra.shape[1:]
    return pl.pallas_call(
        mix_kernel,
        grid=(a, b),
        in_specs=[
            pl.BlockSpec(spectra.shape, lambda i, j: (0, 0, 0)),
            pl.BlockSpec(scales.shape, lambda i, j: (0, 0)),
            pl.BlockSpec((1, 1, mz, 2, c, c), lambda i, j: (i, j, 0, 0, 0, 0)),
        ],
        out_specs=[
            pl.BlockSpec((rows, width), lambda i, j: (0, 0)),
            pl.BlockSpec((1, 1, mz, 2, c, c), lambda i, j: (i, j, 0, 0, 0, 0)),
        ],
        out_shape=[
            jax.ShapeDtypeStruct((rows, width), F32),
            jax.ShapeDtypeStruct((a, b, mz, 2, c, c), F32),
        ],
        scratch_shapes=[
            pltpu.VMEM((rows, width), F32),
            pltpu.VMEM((b, width, c), F32),
            pltpu.VMEM((b, width, c), F32),
        ],
        compiler_params=pltpu.CompilerParams(vmem_limit_bytes=48 * 2**20),
        name="mixing",
    )(spectra, scales, weights)


def synthesis_kernel(scales, m_ref, za_ref, zu_ref, tx_ref, ty_ref, y_ref, u_ref, t_ref, zs_ref):
    groups, lanes, ny = ty_ref.shape
    half = lanes // 2
    space, blk, _, qx, width = m_ref.shape
    my = blk * qx
    per_group, mz = za_ref.shape[0], za_ref.shape[1]
    nx, mx = tx_ref.shape[0], tx_ref.shape[1] // 2
    columns = []
    for s in range(space):
        columns.append(jnp.concatenate([m_ref[s, b, 0] for b in range(blk)], 0))
    spectrum = jnp.concatenate(columns, 1)
    zs_ref[...] = jnp.concatenate([spectrum] * (half // my), 0).T
    for h, (zc_ref, o_ref) in enumerate(((za_ref, y_ref), (zu_ref, u_ref))):
        real = [zs_ref[every(4 * k + 2 * h, mx, 4 * mz), :] for k in range(mz)]
        imag = [zs_ref[every(4 * k + 2 * h + 1, mx, 4 * mz), :] for k in range(mz)]
        for j in range(per_group):
            re = im = None
            for k in range(mz):
                c = zc_ref[j, k, 0:1, :]
                s = zc_ref[j, k, 1:2, :]
                zr = real[k] * c - imag[k] * s
                zi = imag[k] * c + real[k] * s
                re = zr if k == 0 else re + zr
                im = zi if k == 0 else im + zi
            re = re * scales[h]
            im = im * scales[h]
            upper = jnp.concatenate([re, im], 1)
            lower = jnp.concatenate([-im, re], 1)
            block = jnp.concatenate([upper, lower], 0).astype(BF16)
            t_ref[h, j * nx:(j + 1) * nx, :] = dot(tx_ref[...], block).astype(BF16)
        for i in range(groups):
            out = dot(t_ref[h], ty_ref[i]).astype(BF16)
            o_ref[0, i * per_group:(i + 1) * per_group] = out.reshape(per_group, nx, ny)


def synthesize(spectra, za, zu, tx, ty, scales):
    space, blk, c, qx, width = spectra.shape
    per_group, mz, half = za.shape[0], za.shape[1], za.shape[-1]
    groups, _, ny = ty.shape
    nx, mx = tx.shape[0], tx.shape[1] // 2
    nz = per_group * groups
    field = pl.BlockSpec((1, nz, nx, ny), lambda i: (i, 0, 0, 0))
    return pl.pallas_call(
        functools.partial(synthesis_kernel, scales),
        grid=(c,),
        in_specs=[
            pl.BlockSpec((space, blk, 1, qx, width), lambda i: (0, 0, i, 0, 0)),
            pl.BlockSpec(za.shape, lambda i: (0, 0, 0, 0)),
            pl.BlockSpec(zu.shape, lambda i: (0, 0, 0, 0)),
            pl.BlockSpec(tx.shape, lambda i: (0, 0)),
            pl.BlockSpec(ty.shape, lambda i: (0, 0, 0)),
        ],
        out_specs=[field, field],
        out_shape=[jax.ShapeDtypeStruct((c, nz, nx, ny), BF16)] * 2,
        scratch_shapes=[
            pltpu.VMEM((2, per_group * nx, 2 * half), BF16),
            pltpu.VMEM((mx * mz * 4, half), F32),
        ],
        compiler_params=pltpu.CompilerParams(vmem_limit_bytes=48 * 2**20),
        name="synthesis",
    )(spectra, za, zu, tx, ty)


def shards(input_field, cotangent, weights):
    blk_count = lax.axis_size("blk")
    space_count = lax.axis_size("space")
    space_index = lax.axis_index("space")
    c_local, nz_local, nx, ny = input_field.shape
    px, qx, mz = weights.shape[:3]
    mx, my = px * space_count, qx * blk_count
    channels = c_local * blk_count
    nz = nz_local * space_count
    groups = lane_groups(my, nz_local)
    devices = space_count * blk_count
    forward_scale = 1.0 / math.sqrt(nx * ny * nz)
    synth_scale = 1.0 / math.sqrt(mx * my * mz)
    amplitude = np.where(np.arange(mz) == 0, 1.0, 2.0).astype(np.float32)
    ty_in, ty_out = y_tables(ny, my, groups)
    tx_in, tx_out = x_tables(nx, mx)
    zc_unit, zc_amp = z_tables(nz, mz, my, space_count, groups)
    zc_unit = lax.dynamic_index_in_dim(jnp.asarray(zc_unit), space_index, 0, keepdims=False)
    zc_amp = lax.dynamic_index_in_dim(jnp.asarray(zc_amp), space_index, 0, keepdims=False)
    width = px * mz * 4
    sent = (space_count, blk_count, c_local, qx, width)
    scales = np.empty((px, mz, 2, 2, channels), np.float32)
    scales[:, :, 0] = np.float32(forward_scale)
    scales[:, :, 1] = (amplitude * np.float32(synth_scale))[None, :, None, None]
    scales = scales.reshape(width, channels)

    def exchange(send):
        return lax.all_to_all(send, ("space", "blk"), split_axis=0, concat_axis=0, tiled=True)

    parts = analyse(input_field, cotangent, ty_in, tx_in, zc_unit, sent)
    got = exchange(parts.reshape(devices, -1, 128).astype(BF16))
    got = got.reshape(space_count, channels * qx, width)
    mixed, weight_grad = mix(got, scales, weights)

    back = mixed.reshape(1, blk_count, -1, 128).astype(BF16)
    back = jnp.broadcast_to(back, (space_count,) + back.shape[1:])
    home = exchange(back.reshape(devices, -1, 128))
    home = home.astype(F32).reshape(sent)
    spectral_out, field_grad = synthesize(
        home, zc_amp, zc_unit, tx_out, ty_out, (synth_scale, forward_scale)
    )
    return (spectral_out, field_grad, weight_grad)


def solution(mesh):
    placed = (
        P("blk", "space", None, None),
        P("blk", "space", None, None),
        P("space", "blk", None, None, None, None),
    )
    return jax.shard_map(
        shards,
        mesh=mesh,
        in_specs=placed,
        out_specs=placed,
        check_vma=False,
    )
```

time: 204 us -> 119 us (0.58)
  local copies, waits for them, and re-layouts: 66 us -> 4.23 us
  blocking collectives: 41.1 us -> 22.7 us
  waiting for transfers between devices: 0 us -> 14.7 us
  other arithmetic: 14.9 us -> 0.34 us
  Pallas kernels: 79.2 us -> 72.1 us
  starting transfers between devices: 0 us -> 3.08 us
    reshape x5 -> x0, local copies, waits for them, and re-layouts: 22.7 us -> none  [the longest x1 6.05 us: shards(): send = send.reshape(space_count * blk_count, -1, 128)]
    transpose x2 -> x0, local copies, waits for them, and re-layouts: 21.5 us -> none  [the longest x1 17.1 us: shards(): home.transpose(2, 3, 4, 5, 0, 6, 1, 7).reshape(2, c_local, mz, 2, mx, my)]
    all_to_all x2 -> x1, blocking collectives: 41.1 us -> 22.7 us  [exchange(): lax.all_to_all(send, ('space', 'blk'), split_axis=0, concat_axis=0, tiled...]
    all_to_all x0 -> x1, waiting for transfers between devices: none -> 14.7 us  [exchange(): lax.all_to_all(send, ('space', 'blk'), split_axis=0, concat_axis=0, tiled...]
    another operation x4 -> x0, local copies, waits for them, and re-layouts: 7.25 us -> none
    convert_element_type x1 -> x0, local copies, waits for them, and re-layouts: 6.89 us -> none  [shards(): zsum = jnp.sum(got.astype(F32), 0)]
    reduce_sum x1 -> x0, other arithmetic: 6.53 us -> none  [shards(): zsum = jnp.sum(got.astype(F32), 0)]
    pallas_call x2 -> x1, Pallas kernels: 35.9 us -> 32 us  [analyse(): pl.pallas_call(analyse_kernel, grid=(c,), in_specs=[pl.BlockSpec((1, nz,...]
  transfers between devices with their start and end apart: 0 -> 1, of which waited for: 0 -> 1; matrix products, arithmetic and copies ran while one was open for 0% -> 1% of each run, Pallas kernels for 0% -> 0%
where the time goes in v2:
time: 119 us; the launch traced here: 118 us
  Pallas kernels  72.1 us (61%)
  blocking collectives  22.7 us (19%)
  waiting for transfers between devices  14.7 us (12%)
  local copies, waits for them, and re-layouts  4.23 us (4%)
  starting transfers between devices  3.08 us (3%)
    pallas_call x1, Pallas kernels, analyse(): pl.pallas_call(analyse_kernel, grid=(c,), in_specs=[pl.BlockSpec((1, nz,...  32 us
    pallas_call x1, Pallas kernels, synthesize(): pl.pallas_call(functools.partial(synthesis_kernel, scales), grid=(c,), in...  23.6 us
    all_to_all x1, blocking collectives, exchange(): lax.all_to_all(send, ('space', 'blk'), split_axis=0, concat_axis=0, tiled...  22.7 us
    pallas_call x1, Pallas kernels, mix(): pl.pallas_call(mix_kernel, grid=(a, b), in_specs=[pl.BlockSpec(spectra.sh...  16.5 us
    all_to_all x1, waiting for transfers between devices, exchange(): lax.all_to_all(send, ('space', 'blk'), split_axis=0, concat_axis=0, tiled...  14.7 us
    all_to_all x1, starting transfers between devices, exchange(): lax.all_to_all(send, ('space', 'blk'), split_axis=0, concat_axis=0, tiled...  3.08 us
  transfers between devices with their start and end apart: 1, of which 1 were waited for; matrix products, arithmetic and copies ran while one was open for 1% of the time, Pallas kernels for 0%

profile of v2, /device:TPU:0, one launch (start us, length us, event | category | flops | bytes accessed | tf_op | source)
XLA Modules:
  0.0 117.9 jit_solution(17520488055016872840)
XLA Ops:
  0.6 0.8 dynamic-slice_bitcast_fusion.1.zc_ref.zu_ref
  1.4 0.0 copy-start.1
  1.4 1.0 copy-done.1
  2.4 0.0 copy-start.4
  2.4 0.7 copy-done.4
  3.1 0.0 copy-start.2
  3.1 0.0 copy-start
  3.1 0.0 copy-start.3
  3.1 32.0 %analysis.1 = f32[4,8,16,4,128]{4,3,2,1,0:T(4,128)S(1)} custom-call(bf16[16,24,96,192]{3,2,1,0:T(8,128)(2,1)} %f_ref.1, bf16[16,24,96,192]{3,2,1,0:T(8,128)(2,1)} %g_ref.1, bf16[4,192,256]{2,1,0:T(8,128)(2,1)S(1)} %copy-done.1, bf16[32,96]{1,0:T(8,128)(2,1)S(1)} %copy-done.4, f32[6,8,2,128]{3,2,1,0:T(2,128)S(1)} %dynamic-slice_bitcast_fusion.1.zc_ref.zu_ref), custom_call_target="tpu_custom_call" | custom-call | tf_op jit(solution)/shard_map/analysis/pallas_call | solution.py:124
  35.2 0.2 convert_element_type.18
  35.4 22.7 %all_to_all.10 = bf16[32,64,128]{2,1,0:T(8,128)(2,1)S(1)} all-to-all(bf16[32,64,128]{2,1,0:T(8,128)(2,1)S(1)} %bitcast.12), channel_id=1, replica_groups=mesh['blk'=8,'space'=4] {'space','blk'}, dimensions={0} | all-to-all | bytes 1048576 | tf_op jit(solution)/shard_map/all_to_all | solution.py:302
  58.1 0.0 copy-done.2
  58.1 16.5 %mixing.1 = (f32[512,128]{1,0:T(8,128)S(1)}, f32[4,4,8,2,128,128]{5,4,3,2,1,0:T(8,128)}) custom-call(bf16[4,512,128]{2,1,0:T(8,128)(2,1)S(1)} %bitcast.10, f32[128,128]{1,0:T(8,128)S(1)} %copy-done.2, bf16[4,4,8,2,128,128]{5,4,3,2,1,0:T(8,128)(2,1)} %w_ref.1), custom_call_target="tpu_custom_call" | custom-call | tf_op jit(solution)/shard_map/mixing/pallas_call | solution.py:186
  74.6 0.9 broadcast_in_dim.2
  75.5 3.1 %all-to-all-start.1 = ((bf16[32,64,128]{2,1,0:T(8,128)(2,1)}), bf16[32,64,128]{2,1,0:T(8,128)(2,1)S(1)}, u32[]{:S(2)}, u32[]{:S(2)}) async-start(bf16[32,64,128]{2,1,0:T(8,128)(2,1)} %bitcast.4), calls=%async_computation.1 | async-start | bytes 1048576 | tf_op jit(solution)/shard_map/all_to_all | solution.py:302
  78.6 0.8 dynamic-slice_bitcast_fusion.za_ref
  79.4 14.7 %all-to-all-done.1 = bf16[32,64,128]{2,1,0:T(8,128)(2,1)S(1)} async-done(((bf16[32,64,128]{2,1,0:T(8,128)(2,1)}), bf16[32,64,128]{2,1,0:T(8,128)(2,1)S(1)}, u32[]{:S(2)}, u32[]{:S(2)}) %all-to-all-start.1) | async-done | bytes 524320 | tf_op jit(solution)/shard_map/all_to_all | solution.py:302
  94.1 0.1 convert.1.m_ref
  94.2 0.0 copy-done
  94.3 0.0 copy-done.3
  94.3 23.6 %synthesis.1 = (bf16[16,24,96,192]{3,2,1,0:T(8,128)(2,1)}, bf16[16,24,96,192]{3,2,1,0:T(8,128)(2,1)}) custom-call(f32[4,8,16,4,128]{4,3,2,1,0:T(4,128)S(1)} %convert.1.m_ref, f32[6,8,2,128]{3,2,1,0:T(2,128)S(1)} %dynamic-slice_bitcast_fusion.za_ref, f32[6,8,2,128]{3,2,1,0:T(2,128)S(1)} %dynamic-slice_bitcast_fusion.1.zc_ref.zu_ref, ...), custom_call_target="tpu_custom_call" | custom-call | tf_op jit(solution)/shard_map/synthesis/pallas_call | solution.py:254
  (1 shorter events, 0.0 us)
Async XLA Ops:
  1.4 1.0 copy-start.1
  2.4 0.7 copy-start.4
  3.1 54.9 %copy-start.2 = (f32[128,128]{1,0:T(8,128)S(1)}, f32[128,128]{1,0:T(8,128)}, u32[]{:S(2)}) copy-start(f32[128,128]{1,0:T(8,128)} %constant.30.clone.scale_ref) | copy-start | bytes 196612
  3.1 91.1 %copy-start = (bf16[4,256,192]{2,1,0:T(8,128)(2,1)S(1)}, bf16[4,256,192]{2,1,0:T(8,128)(2,1)}, u32[]{:S(2)}) copy-start(bf16[4,256,192]{2,1,0:T(8,128)(2,1)} %constant.32.clone.ty_ref) | copy-start | bytes 1179652
  3.1 91.1 %copy-start.3 = (bf16[96,32]{1,0:T(8,128)(2,1)S(1)}, bf16[96,32]{1,0:T(8,128)(2,1)}, u32[]{:S(2)}) copy-start(bf16[96,32]{1,0:T(8,128)(2,1)} %constant.31.clone.tx_ref) | copy-start | bytes 18436
  75.5 18.6 %all-to-all-start.1 = ((bf16[32,64,128]{2,1,0:T(8,128)(2,1)}), bf16[32,64,128]{2,1,0:T(8,128)(2,1)S(1)}, u32[]{:S(2)}, u32[]{:S(2)}) async-start(bf16[32,64,128]{2,1,0:T(8,128)(2,1)} %bitcast.4), calls=%async_computation.1 | async-start | bytes 1048576 | tf_op jit(solution)/shard_map/all_to_all | solution.py:302

commit v3 on v2

--- a/solution.py
+++ b/solution.py
@@ -71,6 +71,10 @@
 
 def dot(first, second, dims=((1,), (0,))):
     return lax.dot_general(first, second, (dims, ((), ())), preferred_element_type=F32)
+
+
+def estimate(flops, moved):
+    return pl.CostEstimate(flops=int(flops), bytes_accessed=int(moved), transcendentals=0)
 
 
 def every(start, count, stride):
@@ -116,17 +120,17 @@
             o_ref[s, b, 0] = summed[b * qx:(b + 1) * qx, s * width:(s + 1) * width]
 
 
-def analyse(first, second, ty, tx, zc, sent):
-    c, nz, nx, ny = first.shape
+def analyse(first, second, ty, tx, zc, sent, offset):
+    nz, nx, ny = first.shape[1:]
     per_group, mz, half = zc.shape[0], zc.shape[1], zc.shape[-1]
     mx = tx.shape[0] // 2
-    space, blk, _, qx, width = sent
+    space, blk, c, qx, width = sent
     return pl.pallas_call(
         analyse_kernel,
         grid=(c,),
         in_specs=[
-            pl.BlockSpec((1, nz, nx, ny), lambda i: (i, 0, 0, 0)),
-            pl.BlockSpec((1, nz, nx, ny), lambda i: (i, 0, 0, 0)),
+            pl.BlockSpec((1, nz, nx, ny), lambda i: (i + offset, 0, 0, 0)),
+            pl.BlockSpec((1, nz, nx, ny), lambda i: (i + offset, 0, 0, 0)),
             pl.BlockSpec(ty.shape, lambda i: (0, 0, 0)),
             pl.BlockSpec(tx.shape, lambda i: (0, 0)),
             pl.BlockSpec(zc.shape, lambda i: (0, 0, 0, 0)),
@@ -138,22 +142,37 @@
             pltpu.VMEM((mx * mz * 4, half), F32),
         ],
         compiler_params=pltpu.CompilerParams(vmem_limit_bytes=48 * 2**20),
+        cost_estimate=estimate(2 * c * nz * nx * ny * 2 * 256, 4 * c * nz * nx * ny),
         name="analysis",
     )(first, second, ty, tx, zc)
 
 
-def mix_kernel(s_ref, scale_ref, w_ref, o_ref, wg_ref, sum_ref, in_ref, out_ref):
+def pair_rows(x, k, c):
+    fr, fi, gr, gi = (x[4 * k + i:4 * k + i + 1] for i in range(4))
+    row0 = jnp.concatenate([fr, gr, gi], 1)
+    row1 = jnp.concatenate([fi, gi, -gr], 1)
+    both = jnp.concatenate([row0, row1, jnp.zeros((14, 3 * c), F32)], 0).astype(BF16)
+    return both[:, :c], both[:, c:]
+
+
+def mix_kernel(parts, *refs):
+    s_refs, (scale_ref, w_ref) = refs[:parts], refs[parts:parts + 2]
+    o_refs, (in_ref, sum_ref, out_ref) = refs[parts + 2:-3], refs[-3:]
     mz, _, c, _ = w_ref.shape[2:]
     qx = in_ref.shape[0]
+    blk, depth, width = s_refs[0].shape[1:]
     rows = 4 * mz
     a, j = pl.program_id(0), pl.program_id(1)
 
     @pl.when((a == 0) & (j == 0))
     def _():
-        total = s_ref[0].astype(F32)
-        for s in range(1, s_ref.shape[0]):
-            total = total + s_ref[s].astype(F32)
-        sum_ref[...] = total
+        totals = []
+        for s_ref in s_refs:
+            total = s_ref[0].astype(F32)
+            for s in range(1, s_ref.shape[0]):
+                total = total + s_ref[s].astype(F32)
+            totals.append(total)
+        sum_ref[...] = jnp.concatenate(totals, 1).reshape(c * qx, width)
         for i in range(qx):
             in_ref[i] = sum_ref[every(i, c, qx), :].T * scale_ref[...]
 
@@ -161,55 +180,75 @@
     x = in_ref[j, pl.ds(start, rows), :]
     mixed = []
     for k in range(mz):
-        fr, fi, gr, gi = (x[4 * k + i:4 * k + i + 1] for i in range(4))
-        row0 = jnp.concatenate([fr, gr, gi], 1)
-        row1 = jnp.concatenate([fi, gi, -gr], 1)
-        both = jnp.concatenate([row0, row1, jnp.zeros((14, 3 * c), F32)], 0).astype(BF16)
-        f2 = both[:, :c]
-        g2 = both[:, c:]
+        f2, g2 = pair_rows(x, k, c)
         wk = w_ref[0, 0, k].reshape(2 * c, c)
         fm = dot(f2, wk, ((1,), (1,)))
         gm = dot(g2, wk)
         mixed += [fm[0:1, :c] - fm[1:2, c:], fm[1:2, :c] + fm[0:1, c:], gm[0:2]]
-        wg_ref[0, 0, k] = dot(g2, f2, ((0,), (0,))).reshape(2, c, c)
     out_ref[j, pl.ds(start, rows), :] = jnp.concatenate(mixed, 0)
 
     @pl.when((a == pl.num_programs(0) - 1) & (j == pl.num_programs(1) - 1))
     def _():
         for i in range(qx):
-            o_ref[every(i, c, qx), :] = out_ref[i].T
+            sum_ref[every(i, c, qx), :] = out_ref[i].T
+        back = sum_ref[...].reshape(blk, parts * depth, width)
+        for part, o_ref in enumerate(o_refs):
+            piece = back[:, part * depth:(part + 1) * depth].astype(BF16)
+            for s in range(o_ref.shape[0]):
+                o_ref[s] = piece
 
 
 def mix(spectra, scales, weights):
     a, b, mz, _, c, _ = weights.shape
-    rows, width = spectra.shape[1:]
+    sent = spectra[0].shape
+    width = sent[-1]
+    whole = pl.BlockSpec(sent, lambda i, j: (0, 0, 0, 0))
     return pl.pallas_call(
-        mix_kernel,
+        functools.partial(mix_kernel, len(spectra)),
         grid=(a, b),
-        in_specs=[
-            pl.BlockSpec(spectra.shape, lambda i, j: (0, 0, 0)),
+        in_specs=[whole] * len(spectra) + [
             pl.BlockSpec(scales.shape, lambda i, j: (0, 0)),
             pl.BlockSpec((1, 1, mz, 2, c, c), lambda i, j: (i, j, 0, 0, 0, 0)),
         ],
-        out_specs=[
-            pl.BlockSpec((rows, width), lambda i, j: (0, 0)),
-            pl.BlockSpec((1, 1, mz, 2, c, c), lambda i, j: (i, j, 0, 0, 0, 0)),
-        ],
-        out_shape=[
-            jax.ShapeDtypeStruct((rows, width), F32),
-            jax.ShapeDtypeStruct((a, b, mz, 2, c, c), F32),
-        ],
+        out_specs=[whole] * len(spectra) + [pl.BlockSpec((b, width, c), lambda i, j: (0, 0, 0))],
+        out_shape=[jax.ShapeDtypeStruct(sent, BF16)] * len(spectra)
+        + [jax.ShapeDtypeStruct((b, width, c), F32)],
         scratch_shapes=[
-            pltpu.VMEM((rows, width), F32),
+            pltpu.VMEM((c * b, width), F32),
             pltpu.VMEM((b, width, c), F32),
-            pltpu.VMEM((b, width, c), F32),
         ],
         compiler_params=pltpu.CompilerParams(vmem_limit_bytes=48 * 2**20),
+        cost_estimate=estimate(a * b * mz * c * c * 128, 2 * weights.size),
         name="mixing",
-    )(spectra, scales, weights)
-
-
-def synthesis_kernel(scales, m_ref, za_ref, zu_ref, tx_ref, ty_ref, y_ref, u_ref, t_ref, zs_ref):
+    )(*spectra, scales, weights)
+
+
+def outer_kernel(in_ref, wg_ref):
+    mz, _, c, _ = wg_ref.shape[2:]
+    rows = 4 * mz
+    start = pl.multiple_of(pl.program_id(0) * rows, 8)
+    x = in_ref[pl.program_id(1), pl.ds(start, rows), :]
+    for k in range(mz):
+        f2, g2 = pair_rows(x, k, c)
+        wg_ref[0, 0, k] = dot(g2, f2, ((0,), (0,))).reshape(2, c, c)
+
+
+def outer(spectra, shape):
+    a, b, mz, _, c, _ = shape
+    return pl.pallas_call(
+        outer_kernel,
+        grid=(a, b),
+        in_specs=[pl.BlockSpec(spectra.shape, lambda i, j: (0, 0, 0))],
+        out_specs=pl.BlockSpec((1, 1, mz, 2, c, c), lambda i, j: (i, j, 0, 0, 0, 0)),
+        out_shape=jax.ShapeDtypeStruct(shape, F32),
+        compiler_params=pltpu.CompilerParams(vmem_limit_bytes=48 * 2**20),
+        cost_estimate=estimate(a * b * mz * c * c * 64, 8 * a * b * mz * c * c),
+        name="weight_grad",
+    )(spectra)
+
+
+def synthesis_kernel(scales, m_ref, za_ref, zu_ref, tx_ref, ty_ref, *refs):
+    y_ref, u_ref, t_ref, zs_ref = refs[-4:]
     groups, lanes, ny = ty_ref.shape
     half = lanes // 2
     space, blk, _, qx, width = m_ref.shape
@@ -244,13 +283,13 @@
             o_ref[0, i * per_group:(i + 1) * per_group] = out.reshape(per_group, nx, ny)
 
 
-def synthesize(spectra, za, zu, tx, ty, scales):
+def synthesize(spectra, za, zu, tx, ty, scales, channels, offset, earlier):
     space, blk, c, qx, width = spectra.shape
     per_group, mz, half = za.shape[0], za.shape[1], za.shape[-1]
     groups, _, ny = ty.shape
     nx, mx = tx.shape[0], tx.shape[1] // 2
     nz = per_group * groups
-    field = pl.BlockSpec((1, nz, nx, ny), lambda i: (i, 0, 0, 0))
+    field = pl.BlockSpec((1, nz, nx, ny), lambda i: (i + offset, 0, 0, 0))
     return pl.pallas_call(
         functools.partial(synthesis_kernel, scales),
         grid=(c,),
@@ -260,16 +299,18 @@
             pl.BlockSpec(zu.shape, lambda i: (0, 0, 0, 0)),
             pl.BlockSpec(tx.shape, lambda i: (0, 0)),
             pl.BlockSpec(ty.shape, lambda i: (0, 0, 0)),
-        ],
+        ] + [pl.BlockSpec(memory_space=pl.ANY)] * len(earlier),
         out_specs=[field, field],
-        out_shape=[jax.ShapeDtypeStruct((c, nz, nx, ny), BF16)] * 2,
+        out_shape=[jax.ShapeDtypeStruct((channels, nz, nx, ny), BF16)] * 2,
+        input_output_aliases={5 + i: i for i in range(len(earlier))},
         scratch_shapes=[
             pltpu.VMEM((2, per_group * nx, 2 * half), BF16),
             pltpu.VMEM((mx * mz * 4, half), F32),
         ],
         compiler_params=pltpu.CompilerParams(vmem_limit_bytes=48 * 2**20),
+        cost_estimate=estimate(2 * c * nz * nx * ny * 2 * 256, 4 * c * nz * nx * ny),
         name="synthesis",
-    )(spectra, za, zu, tx, ty)
+    )(spectra, za, zu, tx, ty, *earlier)
 
 
 def shards(input_field, cotangent, weights):
@@ -292,7 +333,9 @@
     zc_unit = lax.dynamic_index_in_dim(jnp.asarray(zc_unit), space_index, 0, keepdims=False)
     zc_amp = lax.dynamic_index_in_dim(jnp.asarray(zc_amp), space_index, 0, keepdims=False)
     width = px * mz * 4
-    sent = (space_count, blk_count, c_local, qx, width)
+    halves = 2 if c_local % 2 == 0 else 1
+    c_part = c_local // halves
+    sent = (space_count, blk_count, c_part, qx, width)
     scales = np.empty((px, mz, 2, 2, channels), np.float32)
     scales[:, :, 0] = np.float32(forward_scale)
     scales[:, :, 1] = (amplitude * np.float32(synth_scale))[None, :, None, None]
@@ -301,19 +344,23 @@
     def exchange(send):
         return lax.all_to_all(send, ("space", "blk"), split_axis=0, concat_axis=0, tiled=True)
 
-    parts = analyse(input_field, cotangent, ty_in, tx_in, zc_unit, sent)
-    got = exchange(parts.reshape(devices, -1, 128).astype(BF16))
-    got = got.reshape(space_count, channels * qx, width)
-    mixed, weight_grad = mix(got, scales, weights)
-
-    back = mixed.reshape(1, blk_count, -1, 128).astype(BF16)
-    back = jnp.broadcast_to(back, (space_count,) + back.shape[1:])
-    home = exchange(back.reshape(devices, -1, 128))
-    home = home.astype(F32).reshape(sent)
-    spectral_out, field_grad = synthesize(
-        home, zc_amp, zc_unit, tx_out, ty_out, (synth_scale, forward_scale)
-    )
-    return (spectral_out, field_grad, weight_grad)
+    got = []
+    for part in range(halves):
+        own = analyse(input_field, cotangent, ty_in, tx_in, zc_unit, sent, part * c_part)
+        moved = exchange(own.reshape(devices, c_part * qx, width).astype(BF16))
+        got.append(moved.reshape(space_count, blk_count, c_part * qx, width))
+    *back, spectra = mix(got, scales, weights)
+    weight_grad = outer(spectra, weights.shape)
+
+    outs = ()
+    for part in range(halves):
+        home = exchange(back[part].reshape(devices, c_part * qx, width))
+        home = home.astype(F32).reshape(sent)
+        outs = synthesize(
+            home, zc_amp, zc_unit, tx_out, ty_out, (synth_scale, forward_scale),
+            c_local, part * c_part, outs,
+        )
+    return (outs[0], outs[1], weight_grad)
 
 
 def solution(mesh):

time: 119 us -> 127 us (1.067)
  waiting for transfers between devices: 14.7 us -> 0.01 us
  Pallas kernels: 72.1 us -> 81.9 us
  starting transfers between devices: 3.08 us -> 9.88 us
  blocking collectives: 22.7 us -> 29 us
    all_to_all x1 -> x2, waiting for transfers between devices: 14.7 us -> 0.01 us  [exchange(): lax.all_to_all(send, ('space', 'blk'), split_axis=0, concat_axis=0, tiled...]
    pallas_call x1 -> x2, Pallas kernels: 16.5 us -> 23.5 us  [the longest x1 12.7 us: mix(): pl.pallas_call(functools.partial(mix_kernel, len(spectra)), grid=(a, b),...]
    all_to_all x1 -> x2, starting transfers between devices: 3.08 us -> 9.88 us  [exchange(): lax.all_to_all(send, ('space', 'blk'), split_axis=0, concat_axis=0, tiled...]
    all_to_all x1 -> x2, blocking collectives: 22.7 us -> 29 us  [exchange(): lax.all_to_all(send, ('space', 'blk'), split_axis=0, concat_axis=0, tiled...]
    pallas_call x1 -> x2, Pallas kernels: 32 us -> 33.7 us  [analyse(): pl.pallas_call(analyse_kernel, grid=(c,), in_specs=[pl.BlockSpec((1, nz,...]
    pallas_call x1 -> x2, Pallas kernels: 23.6 us -> 24.6 us  [synthesize(): pl.pallas_call(functools.partial(synthesis_kernel, scales), grid=(c,), in...]
  transfers between devices with their start and end apart: 1 -> 2, of which waited for: 1 -> 0; matrix products, arithmetic and copies ran while one was open for 1% -> 1% of each run, Pallas kernels for 0% -> 22%
where the time goes in v3:
time: 127 us; the launch traced here: 126 us
  Pallas kernels  81.9 us (64%)
  blocking collectives  29 us (23%)
  starting transfers between devices  9.88 us (8%)
  local copies, waits for them, and re-layouts  3.34 us (3%)
    pallas_call x2, Pallas kernels, analyse(): pl.pallas_call(analyse_kernel, grid=(c,), in_specs=[pl.BlockSpec((1, nz,...  33.7 us
    all_to_all x2, blocking collectives, exchange(): lax.all_to_all(send, ('space', 'blk'), split_axis=0, concat_axis=0, tiled...  29 us
    pallas_call x2, Pallas kernels, synthesize(): pl.pallas_call(functools.partial(synthesis_kernel, scales), grid=(c,), in...  24.6 us
    pallas_call x1, Pallas kernels, mix(): pl.pallas_call(functools.partial(mix_kernel, len(spectra)), grid=(a, b),...  12.7 us
    pallas_call x1, Pallas kernels, outer(): pl.pallas_call(outer_kernel, grid=(a, b), in_specs=[pl.BlockSpec(spectra....  10.8 us
    all_to_all x2, starting transfers between devices, exchange(): lax.all_to_all(send, ('space', 'blk'), split_axis=0, concat_axis=0, tiled...  9.88 us
  transfers between devices with their start and end apart: 2, of which 0 were waited for; matrix products, arithmetic and copies ran while one was open for 1% of the time, Pallas kernels for 22%

profile of v3, /device:TPU:0, one launch (start us, length us, event | category | flops | bytes accessed | tf_op | source)
XLA Modules:
  0.0 125.9 jit_solution(1149839665958156626)
XLA Ops:
  0.6 0.8 dynamic-slice_bitcast_fusion.1.zc_ref.zu_ref
  1.4 1.0 copy-done
  2.4 0.7 copy-done.4
  3.1 16.9 %analysis.2 = f32[4,8,8,4,128]{4,3,2,1,0:T(4,128)S(1)} custom-call(bf16[16,24,96,192]{3,2,1,0:T(8,128)(2,1)} %f_ref.3, bf16[16,24,96,192]{3,2,1,0:T(8,128)(2,1)} %g_ref.3, bf16[4,192,256]{2,1,0:T(8,128)(2,1)S(1)} %copy-done, bf16[32,96]{1,0:T(8,128)(2,1)S(1)} %copy-done.4, f32[6,8,2,128]{3,2,1,0:T(2,128)S(1)} %dynamic-slice_bitcast_fusion.1.zc_ref.zu_ref), custom_call_target="tpu_custom_call" | custom-call | flops 3623878656 | bytes 14155776 | tf_op jit(solution)/shard_map/analysis/pallas_call | solution.py:128
  20.0 0.8 convert_element_type.14
  20.8 7.3 %all-to-all-start = ((bf16[32,32,128]{2,1,0:T(8,128)(2,1)}), bf16[32,32,128]{2,1,0:T(8,128)(2,1)S(1)}, u32[]{:S(2)}, u32[]{:S(2)}) async-start(bf16[32,32,128]{2,1,0:T(8,128)(2,1)} %bitcast.1), calls=%async_computation | async-start | bytes 524288 | tf_op jit(solution)/shard_map/all_to_all | solution.py:345
  28.1 0.0 copy-done.1
  28.1 0.0 copy-start.3
  28.1 16.9 %analysis.3 = f32[4,8,8,4,128]{4,3,2,1,0:T(4,128)S(1)} custom-call(bf16[16,24,96,192]{3,2,1,0:T(8,128)(2,1)} %f_ref.3, bf16[16,24,96,192]{3,2,1,0:T(8,128)(2,1)} %g_ref.3, bf16[4,192,256]{2,1,0:T(8,128)(2,1)S(1)} %copy-done.1, bf16[32,96]{1,0:T(8,128)(2,1)S(1)} %copy-done.5, f32[6,8,2,128]{3,2,1,0:T(2,128)S(1)} %dynamic-slice_bitcast_fusion.1.zc_ref.zu_ref), custom_call_target="tpu_custom_call" | custom-call | flops 3623878656 | bytes 14155776 | tf_op jit(solution)/shard_map/analysis/pallas_call | solution.py:128
  45.0 0.0 copy-start.2
  45.0 0.0 copy-start.6
  45.0 0.1 convert_element_type.16
  45.2 0.0 all-to-all-done
  45.2 16.2 %all_to_all.20 = bf16[32,32,128]{2,1,0:T(8,128)(2,1)S(1)} all-to-all(bf16[32,32,128]{2,1,0:T(8,128)(2,1)S(1)} %bitcast.19), channel_id=1, replica_groups=mesh['blk'=8,'space'=4] {'space','blk'}, dimensions={0} | all-to-all | bytes 524288 | tf_op jit(solution)/shard_map/all_to_all | solution.py:345
  61.4 12.7 %mixing.1 = (bf16[4,8,32,128]{3,2,1,0:T(8,128)(2,1)S(1)}, bf16[4,8,32,128]{3,2,1,0:T(8,128)(2,1)}, f32[4,128,128]{2,1,0:T(8,128)S(1)}) custom-call(bf16[4,8,32,128]{3,2,1,0:T(8,128)(2,1)S(1)} %bitcast.14, bf16[4,8,32,128]{3,2,1,0:T(8,128)(2,1)S(1)} %bitcast.15, f32[128,128]{1,0:T(8,128)S(1)} %copy-done.3, bf16[4,4,8,2,128,128]{5,4,3,2,1,0:T(8,128)(2,1)} %refs_3_.1), custom_call_target="tpu_custom_call" | custom-call | flops 268435456 | bytes 8388608 | tf_op jit(solution)/shard_map/mixing/pallas_call | solution.py:206
  74.1 12.8 %all_to_all.21 = bf16[32,32,128]{2,1,0:T(8,128)(2,1)S(1)} all-to-all(bf16[32,32,128]{2,1,0:T(8,128)(2,1)S(1)} %bitcast.16), channel_id=1, replica_groups=mesh['blk'=8,'space'=4] {'space','blk'}, dimensions={0} | all-to-all | bytes 524288 | tf_op jit(solution)/shard_map/all_to_all | solution.py:345
  86.9 2.6 %all-to-all-start.2 = ((bf16[32,32,128]{2,1,0:T(8,128)(2,1)}), bf16[32,32,128]{2,1,0:T(8,128)(2,1)S(1)}, u32[]{:S(2)}, u32[]{:S(2)}) async-start(bf16[32,32,128]{2,1,0:T(8,128)(2,1)} %bitcast.5), calls=%async_computation.2 | async-start | bytes 524288 | tf_op jit(solution)/shard_map/all_to_all | solution.py:345
  89.5 0.8 dynamic-slice_bitcast_fusion.za_ref
  90.3 10.8 %weight_grad.1 = f32[4,4,8,2,128,128]{5,4,3,2,1,0:T(8,128)} custom-call(f32[4,128,128]{2,1,0:T(8,128)S(1)} %get-tuple-element.16.in_ref), custom_call_target="tpu_custom_call" | custom-call | flops 134217728 | bytes 16777216 | tf_op jit(solution)/shard_map/weight_grad/pallas_call | solution.py:238
  101.1 0.1 convert.3.m_ref
  101.2 0.0 all-to-all-done.2
  101.2 0.1 convert.2.m_ref
  101.3 12.3 %synthesis.2 = (bf16[16,24,96,192]{3,2,1,0:T(8,128)(2,1)}, bf16[16,24,96,192]{3,2,1,0:T(8,128)(2,1)}) custom-call(f32[4,8,8,4,128]{4,3,2,1,0:T(4,128)S(1)} %convert.3.m_ref, f32[6,8,2,128]{3,2,1,0:T(2,128)S(1)} %dynamic-slice_bitcast_fusion.za_ref, f32[6,8,2,128]{3,2,1,0:T(2,128)S(1)} %dynamic-slice_bitcast_fusion.1.zc_ref.zu_ref, ...), custom_call_target="tpu_custom_call" | custom-call | flops 3623878656 | bytes 14155776 | tf_op jit(solution)/shard_map/synthesis/pallas_call | solution.py:293
  113.6 12.3 %synthesis.3 = (bf16[16,24,96,192]{3,2,1,0:T(8,128)(2,1)}, bf16[16,24,96,192]{3,2,1,0:T(8,128)(2,1)}) custom-call(f32[4,8,8,4,128]{4,3,2,1,0:T(4,128)S(1)} %convert.2.m_ref, f32[6,8,2,128]{3,2,1,0:T(2,128)S(1)} %dynamic-slice_bitcast_fusion.za_ref, ...), custom_call_target="tpu_custom_call", output_to_operand_aliasing={{0}: (5, {}), {1}: (6, {})} | custom-call | flops 3623878656 | bytes 14155776 | tf_op jit(solution)/shard_map/synthesis/pallas_call | solution.py:293
  (8 shorter events, 0.0 us)
Async XLA Ops:
  1.4 1.0 copy-start
  2.4 0.7 copy-start.4
  3.1 25.0 %copy-start.1 = (bf16[4,192,256]{2,1,0:T(8,128)(2,1)S(1)}, bf16[4,192,256]{2,1,0:T(8,128)(2,1)}, u32[]{:S(2)}) copy-start(bf16[4,192,256]{2,1,0:T(8,128)(2,1)} %constant.28.clone.ty_ref) | copy-start | bytes 1179652
  3.1 25.0 %copy-start.5 = (bf16[32,96]{1,0:T(8,128)(2,1)S(1)}, bf16[32,96]{1,0:T(8,128)(2,1)}, u32[]{:S(2)}) copy-start(bf16[32,96]{1,0:T(8,128)(2,1)} %constant.29.clone.tx_ref) | copy-start | bytes 18436
  20.8 24.4 %all-to-all-start = ((bf16[32,32,128]{2,1,0:T(8,128)(2,1)}), bf16[32,32,128]{2,1,0:T(8,128)(2,1)S(1)}, u32[]{:S(2)}, u32[]{:S(2)}) async-start(bf16[32,32,128]{2,1,0:T(8,128)(2,1)} %bitcast.1), calls=%async_computation | async-start | bytes 524288 | tf_op jit(solution)/shard_map/all_to_all | solution.py:345
  28.1 33.3 %copy-start.3 = (f32[128,128]{1,0:T(8,128)S(1)}, f32[128,128]{1,0:T(8,128)}, u32[]{:S(2)}) copy-start(f32[128,128]{1,0:T(8,128)} %constant.30.clone.refs_2_) | copy-start | bytes 196612
  45.0 56.2 %copy-start.2 = (bf16[4,256,192]{2,1,0:T(8,128)(2,1)S(1)}, bf16[4,256,192]{2,1,0:T(8,128)(2,1)}, u32[]{:S(2)}) copy-start(bf16[4,256,192]{2,1,0:T(8,128)(2,1)} %constant.32.clone.ty_ref) | copy-start | bytes 1179652
  45.0 56.2 %copy-start.6 = (bf16[96,32]{1,0:T(8,128)(2,1)S(1)}, bf16[96,32]{1,0:T(8,128)(2,1)}, u32[]{:S(2)}) copy-start(bf16[96,32]{1,0:T(8,128)(2,1)} %constant.31.clone.tx_ref) | copy-start | bytes 18436
  86.9 14.3 %all-to-all-start.2 = ((bf16[32,32,128]{2,1,0:T(8,128)(2,1)}), bf16[32,32,128]{2,1,0:T(8,128)(2,1)S(1)}, u32[]{:S(2)}, u32[]{:S(2)}) async-start(bf16[32,32,128]{2,1,0:T(8,128)(2,1)} %bitcast.5), calls=%async_computation.2 | async-start | bytes 524288 | tf_op jit(solution)/shard_map/all_to_all | solution.py:345

commit v4 on v3

--- a/solution.py
+++ b/solution.py
@@ -333,8 +333,8 @@
     zc_unit = lax.dynamic_index_in_dim(jnp.asarray(zc_unit), space_index, 0, keepdims=False)
     zc_amp = lax.dynamic_index_in_dim(jnp.asarray(zc_amp), space_index, 0, keepdims=False)
     width = px * mz * 4
-    halves = 2 if c_local % 2 == 0 else 1
-    c_part = c_local // halves
+    pieces = 1
+    c_part = c_local // pieces
     sent = (space_count, blk_count, c_part, qx, width)
     scales = np.empty((px, mz, 2, 2, channels), np.float32)
     scales[:, :, 0] = np.float32(forward_scale)
@@ -345,7 +345,7 @@
         return lax.all_to_all(send, ("space", "blk"), split_axis=0, concat_axis=0, tiled=True)
 
     got = []
-    for part in range(halves):
+    for part in range(pieces):
         own = analyse(input_field, cotangent, ty_in, tx_in, zc_unit, sent, part * c_part)
         moved = exchange(own.reshape(devices, c_part * qx, width).astype(BF16))
         got.append(moved.reshape(space_count, blk_count, c_part * qx, width))
@@ -353,7 +353,7 @@
     weight_grad = outer(spectra, weights.shape)
 
     outs = ()
-    for part in range(halves):
+    for part in range(pieces):
         home = exchange(back[part].reshape(devices, c_part * qx, width))
         home = home.astype(F32).reshape(sent)
         outs = synthesize(

time: 127 us -> 114 us (0.90)
  starting transfers between devices: 9.88 us -> 3.08 us
  blocking collectives: 29 us -> 22.6 us
  waiting for transfers between devices: 0.01 us -> 3.9 us
  Pallas kernels: 81.9 us -> 79.2 us
    all_to_all x2 -> x1, starting transfers between devices: 9.88 us -> 3.08 us  [exchange(): lax.all_to_all(send, ('space', 'blk'), split_axis=0, concat_axis=0, tiled...]
    all_to_all x2 -> x1, blocking collectives: 29 us -> 22.6 us  [exchange(): lax.all_to_all(send, ('space', 'blk'), split_axis=0, concat_axis=0, tiled...]
    all_to_all x2 -> x1, waiting for transfers between devices: 0.01 us -> 3.9 us  [exchange(): lax.all_to_all(send, ('space', 'blk'), split_axis=0, concat_axis=0, tiled...]
    pallas_call x2 -> x1, Pallas kernels: 33.7 us -> 32 us  [analyse(): pl.pallas_call(analyse_kernel, grid=(c,), in_specs=[pl.BlockSpec((1, nz,...]
    pallas_call x2 -> x1, Pallas kernels: 24.6 us -> 23.6 us  [synthesize(): pl.pallas_call(functools.partial(synthesis_kernel, scales), grid=(c,), in...]
  transfers between devices with their start and end apart: 2 -> 1, of which waited for: 0 -> 1; matrix products, arithmetic and copies ran while one was open for 1% -> 1% of each run, Pallas kernels for 22% -> 10%
where the time goes in v4:
time: 114 us; the launch traced here: 113 us
  Pallas kernels  79.2 us (69%)
  blocking collectives  22.6 us (20%)
  waiting for transfers between devices  3.9 us (3%)
  local copies, waits for them, and re-layouts  3.33 us (3%)
  starting transfers between devices  3.08 us (3%)
    pallas_call x1, Pallas kernels, analyse(): pl.pallas_call(analyse_kernel, grid=(c,), in_specs=[pl.BlockSpec((1, nz,...  32 us
    pallas_call x1, Pallas kernels, synthesize(): pl.pallas_call(functools.partial(synthesis_kernel, scales), grid=(c,), in...  23.6 us
    all_to_all x1, blocking collectives, exchange(): lax.all_to_all(send, ('space', 'blk'), split_axis=0, concat_axis=0, tiled...  22.6 us
    pallas_call x1, Pallas kernels, mix(): pl.pallas_call(functools.partial(mix_kernel, len(spectra)), grid=(a, b),...  12.8 us
    pallas_call x1, Pallas kernels, outer(): pl.pallas_call(outer_kernel, grid=(a, b), in_specs=[pl.BlockSpec(spectra....  10.8 us
    all_to_all x1, waiting for transfers between devices, exchange(): lax.all_to_all(send, ('space', 'blk'), split_axis=0, concat_axis=0, tiled...  3.9 us
    all_to_all x1, starting transfers between devices, exchange(): lax.all_to_all(send, ('space', 'blk'), split_axis=0, concat_axis=0, tiled...  3.08 us
  transfers between devices with their start and end apart: 1, of which 1 were waited for; matrix products, arithmetic and copies ran while one was open for 1% of the time, Pallas kernels for 10%

profile of v4, /device:TPU:0, one launch (start us, length us, event | category | flops | bytes accessed | tf_op | source)
XLA Modules:
  0.0 113.2 jit_solution(199813777741987990)
XLA Ops:
  0.6 0.8 dynamic-slice_bitcast_fusion.1.zc_ref.zu_ref
  1.4 0.0 copy-start
  1.4 1.0 copy-done
  2.4 0.0 copy-start.2
  2.4 0.7 copy-done.2
  3.1 0.0 copy-start.1
  3.1 32.0 %analysis.1 = f32[4,8,16,4,128]{4,3,2,1,0:T(4,128)S(1)} custom-call(bf16[16,24,96,192]{3,2,1,0:T(8,128)(2,1)} %f_ref.1, bf16[16,24,96,192]{3,2,1,0:T(8,128)(2,1)} %g_ref.1, bf16[4,192,256]{2,1,0:T(8,128)(2,1)S(1)} %copy-done, bf16[32,96]{1,0:T(8,128)(2,1)S(1)} %copy-done.2, f32[6,8,2,128]{3,2,1,0:T(2,128)S(1)} %dynamic-slice_bitcast_fusion.1.zc_ref.zu_ref), custom_call_target="tpu_custom_call" | custom-call | flops 7247757312 | bytes 28311552 | tf_op jit(solution)/shard_map/analysis/pallas_call | solution.py:128
  35.1 0.0 copy-start.3
  35.2 0.0 copy-start.4
  35.2 0.2 convert_element_type.7
  35.4 22.6 %all_to_all.10 = bf16[32,64,128]{2,1,0:T(8,128)(2,1)S(1)} all-to-all(bf16[32,64,128]{2,1,0:T(8,128)(2,1)S(1)} %bitcast.11), channel_id=1, replica_groups=mesh['blk'=8,'space'=4] {'space','blk'}, dimensions={0} | all-to-all | bytes 1048576 | tf_op jit(solution)/shard_map/all_to_all | solution.py:345
  58.0 0.0 copy-done.1
  58.1 12.8 %mixing.1 = (bf16[4,8,64,128]{3,2,1,0:T(8,128)(2,1)}, f32[4,128,128]{2,1,0:T(8,128)S(1)}) custom-call(bf16[4,8,64,128]{3,2,1,0:T(8,128)(2,1)S(1)} %bitcast.9, f32[128,128]{1,0:T(8,128)S(1)} %copy-done.1, bf16[4,4,8,2,128,128]{5,4,3,2,1,0:T(8,128)(2,1)} %refs_2_.1), custom_call_target="tpu_custom_call" | custom-call | flops 268435456 | bytes 8388608 | tf_op jit(solution)/shard_map/mixing/pallas_call | solution.py:206
  70.8 3.1 %all-to-all-start.1 = ((bf16[32,64,128]{2,1,0:T(8,128)(2,1)}), bf16[32,64,128]{2,1,0:T(8,128)(2,1)S(1)}, u32[]{:S(2)}, u32[]{:S(2)}) async-start(bf16[32,64,128]{2,1,0:T(8,128)(2,1)} %bitcast.3), calls=%async_computation.1 | async-start | bytes 1048576 | tf_op jit(solution)/shard_map/all_to_all | solution.py:345
  73.9 0.8 dynamic-slice_bitcast_fusion.za_ref
  74.7 10.8 %weight_grad.1 = f32[4,4,8,2,128,128]{5,4,3,2,1,0:T(8,128)} custom-call(f32[4,128,128]{2,1,0:T(8,128)S(1)} %get-tuple-element.10.in_ref), custom_call_target="tpu_custom_call" | custom-call | flops 134217728 | bytes 16777216 | tf_op jit(solution)/shard_map/weight_grad/pallas_call | solution.py:238
  85.6 3.9 %all-to-all-done.1 = bf16[32,64,128]{2,1,0:T(8,128)(2,1)S(1)} async-done(((bf16[32,64,128]{2,1,0:T(8,128)(2,1)}), bf16[32,64,128]{2,1,0:T(8,128)(2,1)S(1)}, u32[]{:S(2)}, u32[]{:S(2)}) %all-to-all-start.1) | async-done | bytes 524320 | tf_op jit(solution)/shard_map/all_to_all | solution.py:345
  89.5 0.1 convert.1.m_ref
  89.6 0.0 copy-done.3
  89.6 0.0 copy-done.4
  89.6 23.6 %synthesis.1 = (bf16[16,24,96,192]{3,2,1,0:T(8,128)(2,1)}, bf16[16,24,96,192]{3,2,1,0:T(8,128)(2,1)}) custom-call(f32[4,8,16,4,128]{4,3,2,1,0:T(4,128)S(1)} %convert.1.m_ref, f32[6,8,2,128]{3,2,1,0:T(2,128)S(1)} %dynamic-slice_bitcast_fusion.za_ref, f32[6,8,2,128]{3,2,1,0:T(2,128)S(1)} %dynamic-slice_bitcast_fusion.1.zc_ref.zu_ref, ...), custom_call_target="tpu_custom_call" | custom-call | flops 7247757312 | bytes 28311552 | tf_op jit(solution)/shard_map/synthesis/pallas_call | solution.py:293
Async XLA Ops:
  1.4 1.0 copy-start
  2.4 0.7 copy-start.2
  3.1 54.9 %copy-start.1 = (f32[128,128]{1,0:T(8,128)S(1)}, f32[128,128]{1,0:T(8,128)}, u32[]{:S(2)}) copy-start(f32[128,128]{1,0:T(8,128)} %constant.30.clone.refs_1_) | copy-start | bytes 196612
  35.1 54.4 %copy-start.3 = (bf16[4,256,192]{2,1,0:T(8,128)(2,1)S(1)}, bf16[4,256,192]{2,1,0:T(8,128)(2,1)}, u32[]{:S(2)}) copy-start(bf16[4,256,192]{2,1,0:T(8,128)(2,1)} %constant.32.clone.ty_ref) | copy-start | bytes 1179652
  35.2 54.4 %copy-start.4 = (bf16[96,32]{1,0:T(8,128)(2,1)S(1)}, bf16[96,32]{1,0:T(8,128)(2,1)}, u32[]{:S(2)}) copy-start(bf16[96,32]{1,0:T(8,128)(2,1)} %constant.31.clone.tx_ref) | copy-start | bytes 18436
  70.8 18.6 %all-to-all-start.1 = ((bf16[32,64,128]{2,1,0:T(8,128)(2,1)}), bf16[32,64,128]{2,1,0:T(8,128)(2,1)S(1)}, u32[]{:S(2)}, u32[]{:S(2)}) async-start(bf16[32,64,128]{2,1,0:T(8,128)(2,1)} %bitcast.3), calls=%async_computation.1 | async-start | bytes 1048576 | tf_op jit(solution)/shard_map/all_to_all | solution.py:345
